TPU v7x, 512 devices: a whole 4x8x8 slice. The times are simulated.
512 devices in a mesh: pos: 32 (over y_hi, x, core), chan: 16 (over y_lo, z).
Axes of the slice: x: 4, y: 8 (y_hi: 4, y_lo: 2; y = y_hi * 2 + y_lo), z: 8, core: 2. Of those that a mesh axis runs over, the one named last changes fastest.
Arguments:
- q_in: bfloat16 [4096, 8192], P('pos', 'chan'), may hold values from -6 to 6
- k_in: bfloat16 [4096, 8192], P('pos', 'chan'), may hold values from -6 to 6
- v_in: bfloat16 [4096, 8192], P('pos', 'chan'), may hold values from -6 to 6
- short_weights: float32 [3, 3, 8192], P(None, None, 'chan'), may hold values from -3 to 3
- residues: float32 [8192, 16], P('chan')
- log_decay: float32 [8192, 16], P('chan')
- out_weight: bfloat16 [8192, 8192], P('chan', 'pos'), may hold values from -0.0625 to 0.0625
- grad_out: bfloat16 [4096, 8192], P(('pos', 'chan')), may hold values from -6 to 6
Outputs:
- grad_q: bfloat16 [4096, 8192], P('pos', 'chan')
- grad_k: bfloat16 [4096, 8192], P('pos', 'chan')
- grad_v: bfloat16 [4096, 8192], P('pos', 'chan')
- grad_short: float32 [3, 3, 8192], P(None, None, 'chan')
- grad_residues: float32 [8192, 16], P('chan')
- grad_log_decay: float32 [8192, 16], P('chan')
All inputs are finite; a program needn't handle non-finite values.
Results may differ from a plain program's by a relative error of at most 0.029.
Values may be sent and summed in bfloat16 or wider, within the bound.
A program may use at most 64 MiB of HBM per device.

v0:
```python
import math

import jax
import jax.numpy as jnp
from jax import lax
from jax.sharding import PartitionSpec as P

INNER = 128


HIGHEST = lax.Precision.HIGHEST


def passed_along(block, axis, distance):
    devices = range(lax.axis_size(axis))
    route = [(i - distance, i) for i in devices if i - distance in devices]
    return lax.ppermute(block, axis, route)


def decay_tables(rate, base, width, blocks):
    near_times = jnp.arange(width).astype(jnp.float32)
    far_times = base + (jnp.arange(blocks) * width).astype(jnp.float32)
    near = jnp.exp(-rate[:, :, None] * near_times[None, None, :])
    far = jnp.exp(-rate[:, :, None] * far_times[None, None, :])
    return (near, far, near_times, far_times)


def filter_taps(residue, rate, total, width):
    blocks = total // width
    near, far, near_times, far_times = decay_tables(rate, jnp.float32(0.0), width, blocks)
    scaled = residue[:, :, None] * far
    taps = jnp.einsum("cna,cnb->cab", scaled, near, precision=HIGHEST)
    return taps.reshape(residue.shape[0], total)


def mode_sums(grad_taps, residue, rate, base, width):
    channel_count = grad_taps.shape[0]
    blocks = grad_taps.shape[1] // width
    near, far, near_times, far_times = decay_tables(rate, base, width, blocks)
    pieces = grad_taps.reshape(channel_count, blocks, width)
    plain = jnp.einsum("cab,cnb->cna", pieces, near, precision=HIGHEST)
    timed = jnp.einsum("cab,cnb->cna", pieces, near * near_times[None, None, :], precision=HIGHEST)
    by_residue = jnp.sum(far * plain, axis=2)
    moment = jnp.sum(far * (far_times[None, None, :] * plain + timed), axis=2)
    return (by_residue, -moment * residue * rate)


def dft_tables(outer, inner):
    length = outer * inner
    half_rows = jnp.arange(outer // 2, dtype=jnp.int32)
    outer_freq = jnp.arange(outer, dtype=jnp.int32)
    inner_index = jnp.arange(inner, dtype=jnp.int32)
    first = (
        2.0
        * math.pi
        / outer
        * (half_rows[:, None] * outer_freq[None, :] % outer).astype(jnp.float32)
    )
    twist = (
        2.0
        * math.pi
        / length
        * (outer_freq[:, None] * inner_index[None, :] % length).astype(jnp.float32)
    )
    second = (
        2.0
        * math.pi
        / inner
        * (inner_index[:, None] * inner_index[None, :] % inner).astype(jnp.float32)
    )
    return (
        jnp.cos(first),
        jnp.sin(first),
        jnp.cos(twist),
        jnp.sin(twist),
        jnp.cos(second),
        jnp.sin(second),
    )


def forward_dft(signal, tables):
    cos_a, sin_a, cos_t, sin_t, cos_b, sin_b = tables
    channel_count = signal.shape[0]
    blocks = signal.reshape(channel_count, cos_a.shape[0], cos_b.shape[0])
    part_re = jnp.einsum("cnb,nk->ckb", blocks, cos_a, precision=HIGHEST)
    part_im = -jnp.einsum("cnb,nk->ckb", blocks, sin_a, precision=HIGHEST)
    turned_re = part_re * cos_t + part_im * sin_t
    turned_im = part_im * cos_t - part_re * sin_t
    spec_re = jnp.einsum("ckb,bm->ckm", turned_re, cos_b, precision=HIGHEST) + jnp.einsum(
        "ckb,bm->ckm", turned_im, sin_b, precision=HIGHEST
    )
    spec_im = jnp.einsum("ckb,bm->ckm", turned_im, cos_b, precision=HIGHEST) - jnp.einsum(
        "ckb,bm->ckm", turned_re, sin_b, precision=HIGHEST
    )
    return (spec_re, spec_im)


def inverse_dft(spec_re, spec_im, tables):
    cos_a, sin_a, cos_t, sin_t, cos_b, sin_b = tables
    channel_count = spec_re.shape[0]
    back_re = jnp.einsum("ckb,bm->ckm", spec_re, cos_b, precision=HIGHEST) - jnp.einsum(
        "ckb,bm->ckm", spec_im, sin_b, precision=HIGHEST
    )
    back_im = jnp.einsum("ckb,bm->ckm", spec_re, sin_b, precision=HIGHEST) + jnp.einsum(
        "ckb,bm->ckm", spec_im, cos_b, precision=HIGHEST
    )
    turned_re = back_re * cos_t - back_im * sin_t
    turned_im = back_re * sin_t + back_im * cos_t
    signal = jnp.einsum("ckb,nk->cnb", turned_re, cos_a, precision=HIGHEST) - jnp.einsum(
        "ckb,nk->cnb", turned_im, sin_a, precision=HIGHEST
    )
    scale = 1.0 / (cos_a.shape[1] * cos_b.shape[0])
    return signal.reshape(channel_count, -1) * scale


def local(q_in, k_in, v_in, short_weights, residues, log_decay, out_weight, grad_out):
    local_rows = q_in.shape[0]
    local_chans = q_in.shape[1]
    positions_count = lax.axis_size("pos")
    spec_chans = local_chans // positions_count
    sequence = local_rows * positions_count
    taps_count = short_weights.shape[1]
    streams = jnp.stack([q_in, k_in, v_in]).transpose(0, 2, 1)
    before = passed_along(streams[:, :, local_rows - (taps_count - 1) :], "pos", 1)
    extended = jnp.concatenate([before, streams], axis=2).astype(jnp.float32)
    conv = sum(
        (
            short_weights[:, lag, :, None]
            * extended[:, :, taps_count - 1 - lag : taps_count - 1 - lag + local_rows]
            for lag in range(taps_count)
        )
    )
    q_conv = conv[0].astype(jnp.bfloat16)
    k_conv = conv[1]
    v_conv = conv[2]
    gated = (k_conv * v_conv).astype(jnp.bfloat16)
    token_grads = lax.all_gather(grad_out, "chan", axis=0, tiled=True)
    grad_mix = lax.dot_general(
        lax.all_gather(out_weight, "pos", axis=1, tiled=True),
        token_grads,
        (((1,), (1,)), ((), ())),
        preferred_element_type=jnp.float32,
    ).astype(jnp.bfloat16)
    offset = lax.axis_index("pos") * spec_chans
    own_residues = lax.dynamic_slice_in_dim(residues, offset, spec_chans, 0)
    own_rates = jnp.exp(lax.dynamic_slice_in_dim(log_decay, offset, spec_chans, 0))
    whole_width = math.gcd(sequence, 128)
    tables = dft_tables(2 * sequence // INNER, INNER)
    taps_re, taps_im = forward_dft(
        filter_taps(own_residues, own_rates, sequence, whole_width), tables
    )
    sent = lax.all_to_all(gated[None], "pos", split_axis=1, concat_axis=2, tiled=True)
    gated_re, gated_im = forward_dft(sent[0].astype(jnp.float32), tables)
    filtered_whole = inverse_dft(
        taps_re * gated_re - taps_im * gated_im, taps_re * gated_im + taps_im * gated_re, tables
    )
    filtered = lax.all_to_all(filtered_whole[None], "pos", split_axis=2, concat_axis=1, tiled=True)[
        0
    ]
    mix = grad_mix.astype(jnp.float32)
    grad_q_conv = mix * filtered
    gate_grad = (mix * q_conv.astype(jnp.float32)).astype(jnp.bfloat16)
    grad_filtered = lax.all_to_all(gate_grad[None], "pos", split_axis=1, concat_axis=2, tiled=True)[
        0
    ]
    grad_re, grad_im = forward_dft(grad_filtered.astype(jnp.float32), tables)
    grad_gated_whole = inverse_dft(
        taps_re * grad_re + taps_im * grad_im, taps_re * grad_im - taps_im * grad_re, tables
    )
    grad_taps = inverse_dft(
        grad_re * gated_re + grad_im * gated_im, grad_im * gated_re - grad_re * gated_im, tables
    )
    returned = [grad_gated_whole]
    returned = returned + [grad_taps]
    back = lax.all_to_all(jnp.stack(returned), "pos", split_axis=2, concat_axis=1, tiled=True)
    grad_gated = back[0]
    grad_streams = jnp.stack([grad_q_conv, grad_gated * v_conv, grad_gated * k_conv])
    after = passed_along(grad_streams[:, :, : taps_count - 1], "pos", -1)
    grad_extended = jnp.concatenate([grad_streams, after], axis=2)
    grad_inputs = sum(
        (
            short_weights[:, lag, :, None] * grad_extended[:, :, lag : lag + local_rows]
            for lag in range(taps_count)
        )
    ).astype(jnp.bfloat16)
    short_part = jnp.stack(
        [
            jnp.sum(
                grad_streams
                * extended[:, :, taps_count - 1 - lag : taps_count - 1 - lag + local_rows],
                axis=2,
            )
            for lag in range(taps_count)
        ],
        axis=1,
    )
    local_start = (lax.axis_index("pos") * local_rows).astype(jnp.float32)
    local_width = math.gcd(local_rows, 16)
    part_residue, part_rate = mode_sums(
        back[-1], residues, jnp.exp(log_decay), local_start, local_width
    )
    grad_short, grad_residues, grad_rates = (
        lax.psum(short_part.astype(jnp.bfloat16), "pos").astype(jnp.float32),
        lax.psum(part_residue.astype(jnp.bfloat16), "pos").astype(jnp.float32),
        lax.psum(part_rate.astype(jnp.bfloat16), "pos").astype(jnp.float32),
    )
    return (
        grad_inputs[0].T,
        grad_inputs[1].T,
        grad_inputs[2].T,
        grad_short,
        grad_residues,
        grad_rates,
    )


def solution(mesh):
    in_specs = (
        P("pos", "chan"),
        P("pos", "chan"),
        P("pos", "chan"),
        P(None, None, "chan"),
        P("chan", None),
        P("chan", None),
        P("chan", "pos"),
        P(("pos", "chan"), None),
    )
    out_specs = (
        P("pos", "chan"),
        P("pos", "chan"),
        P("pos", "chan"),
        P(None, None, "chan"),
        P("chan", None),
        P("chan", None),
    )
    return jax.shard_map(local, mesh=mesh, in_specs=in_specs, out_specs=out_specs, check_vma=False)
```

profile of v0, /device:TPU:1, one launch (start us, length us, event | category | flops | bytes accessed | tf_op | source)
XLA Modules:
  0.0 488.9 jit_solution(16231826074750958963)
XLA Ops:
  8.7 1.1 maximum_bitcast_fusion
  9.7 4.5 collective-permute-start
  15.4 0.9 fusion.342
  18.4 0.8 fusion.35
  19.2 1.6 convolution_add_fusion.5
  21.3 0.9 copy-done
  22.9 1.4 reduce
  25.0 9.9 %all-to-all-start = ((bf16[32,2,1024]{2,1,0:T(2,128)(2,1)}), bf16[32,2,1024]{2,1,0:T(2,128)(2,1)S(1)}, u32[]{:S(2)}, u32[]{:S(2)}) async-start(bf16[32,2,1024]{2,1,0:T(2,128)(2,1)} %reshape.143), calls=%async_computation | async-start | bytes 262144 | tf_op jit(solution)/shard_map/all_to_all | solution.py:152
  34.9 0.8 fusion.31
  35.7 11.1 %all-to-all-done = bf16[32,2,1024]{2,1,0:T(2,128)(2,1)S(1)} async-done(((bf16[32,2,1024]{2,1,0:T(2,128)(2,1)}), bf16[32,2,1024]{2,1,0:T(2,128)(2,1)S(1)}, u32[]{:S(2)}, u32[]{:S(2)}) %all-to-all-start) | async-done | bytes 131104 | tf_op jit(solution)/shard_map/all_to_all | solution.py:152
  48.0 0.8 fusion.25
  48.8 1.6 fusion.29
  50.5 1.6 convolution_subtract_fusion.4
  52.1 30.6 %all-gather.5.cloned.1.call-done = bf16[128,8192]{1,0:T(8,128)(2,1)} async-done(((bf16[8,8192]{1,0:T(8,128)(2,1)}), bf16[128,8192]{1,0:T(8,128)(2,1)}) %all-gather.5.cloned.1.call-update) | async-done | bytes 2097168 | tf_op jit(solution)/shard_map/all_gather | solution.py:137
  82.7 100.4 %all-gather.3.cloned.1.call-done = bf16[512,8192]{1,0:T(8,128)(2,1)} async-done(((bf16[512,256]{1,0:T(8,128)(2,1)}), bf16[512,8192]{1,0:T(8,128)(2,1)}) %all-gather.3.cloned.1.call-update) | async-done | bytes 8388624 | tf_op jit(solution)/shard_map/all_gather | solution.py:139
  183.1 6.9 %fusion.15 = f32[512,128]{0,1:T(8,128)S(1)} fusion(bf16[512,8192]{1,0:T(8,128)(2,1)} %all-gather.3.cloned.1.call-done, bf16[128,8192]{1,0:T(8,128)(2,1)} %all-gather.5.cloned.1.call-done), kind=kOutput, calls=%fused_computation.36 | convolution fusion | flops 1073872896 | bytes 10747904 | tf_op jit(solution)/shard_map/dot_general | solution.py:138
  190.8 1.6 fusion.71
  192.4 1.8 copy.93
  194.2 3.0 reduce.1
  197.1 1.6 reshape.141
  198.7 6.2 %all-to-all-start.2 = ((bf16[32,2,1024]{2,1,0:T(2,128)(2,1)}), bf16[32,2,1024]{2,1,0:T(2,128)(2,1)}, u32[]{:S(2)}, u32[]{:S(2)}) async-start(bf16[32,2,1024]{2,1,0:T(2,128)(2,1)} %reshape.141), calls=%async_computation.2 | async-start | bytes 262144 | tf_op jit(solution)/shard_map/all_to_all | solution.py:163
  204.9 2.7 convolution_add_fusion.4
  207.6 8.7 %all-to-all-done.2 = bf16[32,2,1024]{2,1,0:T(2,128)(2,1)} async-done(((bf16[32,2,1024]{2,1,0:T(2,128)(2,1)}), bf16[32,2,1024]{2,1,0:T(2,128)(2,1)}, u32[]{:S(2)}, u32[]{:S(2)}) %all-to-all-start.2) | async-done | bytes 131104 | tf_op jit(solution)/shard_map/all_to_all | solution.py:163
  216.3 1.9 reshape.142
  219.3 0.8 fusion.19
  220.1 0.8 fusion.23
  220.9 0.8 convolution_subtract_fusion.2
  221.8 0.8 convolution_add_fusion.2
  222.6 1.1 multiply_add_fusion.4
  223.8 0.8 fusion.100
  224.6 0.8 fusion.116
  225.4 0.8 fusion.92
  226.2 0.8 fusion.108
  227.0 0.8 fusion.95
  228.7 0.8 convolution_add_fusion.3
  229.5 0.8 convolution_subtract_fusion.3
  231.0 1.2 fusion.14
  232.2 0.8 convolution_add_fusion
  233.1 0.8 convolution_subtract_fusion
  234.4 1.2 fusion.10
  235.6 0.8 convolution_add_fusion.1
  236.4 1.6 convolution_subtract_fusion.1
  238.1 1.6 copy.106
  240.1 19.4 %reduce.3 = f32[4096,16]{1,0:T(8,128)} reduce(f32[4096,1,16]{2,1,0:T(1,128)S(1)} %bitcast.213, f32[]{:T(128)} %broadcast.268), dimensions={1}, to_apply=%bitcast.185.reduce_sub_computation | reduce | bytes 524292
  259.5 3.0 reshape.147
  262.6 4.2 all-to-all-start.1
  267.9 4.4 copy.95
  272.3 8.0 %reshape.145 = f32[32,1,4096]{2,1,0:T(1,128)} reshape(f32[4096,2,16]{2,1,0:T(2,128)} %bitcast.210) | data formatting | bytes 1048576
  280.3 9.9 %all-to-all-start.3 = ((f32[32,1,4096]{2,1,0:T(1,128)}), f32[32,1,4096]{2,1,0:T(1,128)S(1)}, u32[]{:S(2)}, u32[]{:S(2)}) async-start(f32[32,1,4096]{2,1,0:T(1,128)} %reshape.145), calls=%async_computation.3 | async-start | bytes 1048576 | tf_op jit(solution)/shard_map/all_to_all | solution.py:175
  290.2 0.9 copy.100
  291.1 2.0 reduce.4
  293.0 4.9 %reshape.148 = f32[4096,1,16]{2,1,0:T(1,128)S(1)} reshape(f32[32,2048]{1,0:T(8,128)} %reduce.4) | data formatting | bytes 524288
  297.9 3.5 copy.90
  301.5 1.1 copy.91
  302.7 1.0 multiply_bitcast_fusion
  303.7 4.9 %all-to-all-done.3 = f32[32,1,4096]{2,1,0:T(1,128)S(1)} async-done(((f32[32,1,4096]{2,1,0:T(1,128)}), f32[32,1,4096]{2,1,0:T(1,128)S(1)}, u32[]{:S(2)}, u32[]{:S(2)}) %all-to-all-start.3) | async-done | bytes 524320 | tf_op jit(solution)/shard_map/all_to_all | solution.py:175
  308.6 1.9 reduce.2
  310.5 6.9 %reshape.146 = f32[4096,2,16]{2,1,0:T(2,128)} reshape(f32[32,4096]{1,0:T(8,128)S(1)} %reduce.2) | data formatting | bytes 1048576
  317.5 3.5 copy.107
  322.2 2.3 collective-permute-start.1
  324.6 1.9 reshape_squeeze.3
  326.5 9.0 %multiply_reduce_fusion.1 = (bf16[512,16]{1,0:T(8,128)(2,1)S(1)}, f32[512,16,8]{1,2,0:T(8,128)S(1)}) fusion(f32[8]{0:T(128)S(1)} %convert_add_fusion, f32[512,16]{1,0:T(8,128)S(1)} %copy-done.9, f32[512,8,16]{2,1,0:T(8,128)} %reshape_squeeze.3, f32[16]{0:T(128)S(1)} %iota_convert_fusion), kind=kOutput, calls=%fused_computation.5 | convolution fusion | flops 12902400 | bytes 573536 | tf_op jit(solution)/shard_map/cab,cnb->cna/dot_general | solution.py:41
  335.6 7.6 %multiply_reduce_fusion = f32[512,16]{1,0:T(8,128)S(1)} fusion(f32[512,16,8]{1,2,0:T(8,128)S(1)} %get-tuple-element.58, f32[512,8,16]{2,1,0:T(8,128)S(1)} %copy-done.6, f32[16]{0:T(128)S(1)} %iota_convert_fusion, f32[512,16]{1,0:T(8,128)S(1)} %copy-done.9, f32[8]{0:T(128)S(1)} %convert_add_fusion), kind=kOutput, calls=%fused_computation.4 | convolution fusion | flops 13164544 | bytes 589920 | tf_op jit(solution)/shard_map/cab,cnb->cna/dot_general | solution.py:42
  344.7 135.3 %all-reduce = (bf16[3,3,512]{2,0,1:T(4,128)(2,1)S(1)}, bf16[512,16]{1,0:T(8,128)(2,1)S(1)}, bf16[512,16]{0,1:T(8,128)(2,1)S(1)}) all-reduce(bf16[3,3,512]{2,0,1:T(4,128)(2,1)S(1)} %pad_maximum_fusion.3, bf16[512,16]{1,0:T(8,128)(2,1)S(1)} %get-tuple-element.57, ...), channel_id=1, replica_groups=mesh['pos'=32,'chan'=16] {'pos'}, use_global_device_ids=true, to_apply=%region_3.4 | all-reduce | flops 20992 | bytes 83968 | tf_op jit(solution)/shard_map/psum | solution.py:203
  (84 shorter events, 17.8 us)
Async XLA Ops:
  7.2 75.6 %all-gather.5.cloned.1.call-start = ((), (), s32[]{:S(2)}) async-start(), calls=%async_computation.5 | async-start | bytes 2228224 | tf_op jit(solution)/shard_map/all_gather | solution.py:137
  7.9 175.2 %all-gather.3.cloned.1.call-start = ((), (), s32[]{:S(2)}) async-start(), calls=%async_computation.4 | async-start | bytes 8650752 | tf_op jit(solution)/shard_map/all_gather | solution.py:139
  9.7 11.1 %collective-permute-start = (bf16[3,512,2]{1,2,0:T(2,128)(2,1)S(1)}, bf16[3,512,2]{1,2,0:T(2,128)(2,1)S(1)}, u32[]{:S(2)}, u32[]{:S(2)}) collective-permute-start(bf16[3,512,2]{1,2,0:T(2,128)(2,1)S(1)} %slice.81), channel_id=1, source_target_pairs={{0,16},{16,32},{32,48},{48,64},{64,80},{80,96},{96,112},{112,128},... | collective-permute-start | bytes 18440 | tf_op jit(solution)/shard_map/ppermute | solution.py:17
  21.3 0.9 copy-start
  25.0 21.9 %all-to-all-start = ((bf16[32,2,1024]{2,1,0:T(2,128)(2,1)}), bf16[32,2,1024]{2,1,0:T(2,128)(2,1)S(1)}, u32[]{:S(2)}, u32[]{:S(2)}) async-start(bf16[32,2,1024]{2,1,0:T(2,128)(2,1)} %reshape.143), calls=%async_computation | async-start | bytes 262144 | tf_op jit(solution)/shard_map/all_to_all | solution.py:152
  190.0 0.7 copy-start.7
  198.7 17.6 %all-to-all-start.2 = ((bf16[32,2,1024]{2,1,0:T(2,128)(2,1)}), bf16[32,2,1024]{2,1,0:T(2,128)(2,1)}, u32[]{:S(2)}, u32[]{:S(2)}) async-start(bf16[32,2,1024]{2,1,0:T(2,128)(2,1)} %reshape.141), calls=%async_computation.2 | async-start | bytes 262144 | tf_op jit(solution)/shard_map/all_to_all | solution.py:163
  220.9 1.7 copy-start.3
  220.9 1.7 copy-start.4
  220.9 1.7 copy-start.5
  259.5 7.2 %copy-start.2 = (f32[16,64,128]{2,1,0:T(8,128)S(1)}, f32[16,64,128]{2,1,0:T(8,128)}, u32[]{:S(2)}) copy-start(f32[16,64,128]{2,1,0:T(8,128)} %convolution_subtract_fusion.1) | copy-start | bytes 1572868
  262.6 5.2 %copy-start.8 = (f32[16,32,128]{2,1,0:T(8,128)S(1)}, f32[16,32,128]{2,1,0:T(8,128)}, u32[]{:S(2)}) copy-start(f32[16,32,128]{2,1,0:T(8,128)} %fusion.10) | copy-start | bytes 786436
  262.6 17.7 %all-to-all-start.1 = ((f32[32,1,2048]{2,1,0:T(1,128)}), f32[32,1,2048]{2,1,0:T(1,128)S(1)}, u32[]{:S(2)}, u32[]{:S(2)}) async-start(f32[32,1,2048]{2,1,0:T(1,128)} %reshape.147), calls=%async_computation.1 | async-start | bytes 524288 | tf_op jit(solution)/shard_map/all_to_all | solution.py:157
  272.3 17.9 %copy-start.10 = (f32[512,16]{0,1:T(8,128)S(1)}, f32[512,16]{0,1:T(8,128)}, u32[]{:S(2)}) copy-start(f32[512,16]{0,1:T(8,128)} %param.13) | copy-start | bytes 98308
  280.3 28.4 %all-to-all-start.3 = ((f32[32,1,4096]{2,1,0:T(1,128)}), f32[32,1,4096]{2,1,0:T(1,128)S(1)}, u32[]{:S(2)}, u32[]{:S(2)}) async-start(f32[32,1,4096]{2,1,0:T(1,128)} %reshape.145), calls=%async_computation.3 | async-start | bytes 1048576 | tf_op jit(solution)/shard_map/all_to_all | solution.py:175
  320.9 1.1 copy-start.1
  322.1 4.4 copy-start.9
  322.2 21.1 %collective-permute-start.1 = (f32[3,512,2]{1,2,0:T(2,128)S(1)}, f32[3,512,2]{1,2,0:T(2,128)S(1)}, u32[]{:S(2)}, u32[]{:S(2)}) collective-permute-start(f32[3,512,2]{1,2,0:T(2,128)S(1)} %slice.89), channel_id=1, source_target_pairs={{16,0},{32,16},{48,32},{64,48},{80,64},{96,80},{112,96},{128,112},... | collective-permute-start | bytes 36872 | tf_op jit(solution)/shard_map/ppermute | solution.py:17
  326.5 9.0 %copy-start.6 = (f32[512,8,16]{2,1,0:T(8,128)S(1)}, f32[512,8,16]{2,1,0:T(8,128)}, u32[]{:S(2)}) copy-start(f32[512,8,16]{2,1,0:T(8,128)} %reshape_squeeze.3) | copy-start | bytes 786436
  335.6 7.7 %copy-start.11 = (f32[512,16]{0,1:T(8,128)S(1)}, f32[512,16]{0,1:T(8,128)}, u32[]{:S(2)}) copy-start(f32[512,16]{0,1:T(8,128)} %param.12) | copy-start | bytes 98308
Sparse Core Ops, SparseCore 0:
  10.1 72.6 all-gather.4
  85.8 97.2 all-gather.2
where the time goes:
time: 499 us; the launch traced here: 489 us
  waiting for transfers between devices  157 us (31%)
  blocking collectives  135 us (27%)
  matrix products  57.3 us (11%)
  local copies, waits for them, and re-layouts  53.1 us (11%)
  starting transfers between devices  37.1 us (7%)
  other arithmetic  34.1 us (7%)
  between operations  14.9 us (3%)
    psum x1, blocking collectives, local(): lax.psum(short_part.astype(jnp.bfloat16), 'pos').astype(jnp.float32)  135 us
    all_gather x1, waiting for transfers between devices, local(): lax.all_gather(out_weight, 'pos', axis=1, tiled=True)  100 us
    unnamed x39, local copies, waits for them, and re-layouts  31.2 us
    all_gather x1, waiting for transfers between devices, local(): token_grads = lax.all_gather(grad_out, 'chan', axis=0, tiled=True)  30.6 us
    unnamed x3, other arithmetic  23.8 us
    all_to_all x1, waiting for transfers between devices, local(): lax.all_to_all(gated[None], 'pos', split_axis=1, concat_axis=2, tiled=True)  11.1 us
  transfers between devices with their start and end apart: 8, of which 5 were waited for; matrix products, arithmetic and copies ran while one was open for 13% of the time, Pallas kernels for 0%

commit v1 on v0

v1 whole, which is shorter than its diff:
```python
import functools

import jax
import jax.numpy as jnp
from jax import lax
from jax.experimental import pallas as pl
from jax.experimental.pallas import tpu as pltpu
from jax.sharding import PartitionSpec as P

F32 = jnp.float32
BF16 = jnp.bfloat16
MESH = pl.DeviceIdType.MESH

YH, XN, CORES = 4, 4, 2
YL, ZN = 2, 8
POS = YH * XN * CORES
CHAN = YL * ZN
ROW = XN * CORES
BLK = 128
OWN = 16
MODES = 16
TAPS = 3


def remote(src, dst, send, recv, **device):
    return pltpu.make_async_remote_copy(
        src_ref=src, dst_ref=dst, send_sem=send, recv_sem=recv,
        device_id=device, device_id_type=MESH,
    )


def full(memory=pltpu.VMEM):
    return pl.BlockSpec(memory_space=memory)


def later(x, j):
    if j == 0:
        return x
    lane = lax.broadcasted_iota(jnp.int32, x.shape, 2)
    turned = pltpu.roll(x, j, 2)
    before = jnp.concatenate([jnp.zeros_like(turned[:1]), turned[:-1]], axis=0)
    return jnp.where(lane < j, before, turned)


def sooner(x, j):
    if j == 0:
        return x
    lane = lax.broadcasted_iota(jnp.int32, x.shape, 2)
    turned = pltpu.roll(x, BLK - j, 2)
    after = jnp.concatenate([turned[1:], jnp.zeros_like(turned[:1])], axis=0)
    return jnp.where(lane >= BLK - j, after, turned)


def halves(x):
    high = x.astype(BF16)
    return high, (x - high.astype(F32)).astype(BF16)


def dot(a, b, da, db):
    return lax.dot_general(a, b, (((da,), (db,)), ((), ())), preferred_element_type=F32)


def mixer_kernel(qkv, gm, sw, res, ld, out, small, xs, xr, gs, fs, gg, up, vp, cd):
    me = lax.axis_index("pos")
    first = me * OWN
    chans = sw.shape[2]
    pick = lax.broadcasted_iota(jnp.int32, (OWN, chans), 1) == (
        first + lax.broadcasted_iota(jnp.int32, (OWN, chans), 0)
    )
    cols = [
        [
            jnp.sum(jnp.where(pick, sw[s, pl.ds(j, 1), :], 0.0), axis=1, keepdims=True)[None]
            for j in range(TAPS)
        ]
        for s in range(3)
    ]
    streams = [qkv[:, s].astype(F32) for s in range(3)]

    def conv(s):
        return sum(cols[s][j] * later(streams[s], j) for j in range(TAPS))

    kc, vc = conv(1), conv(2)
    rows = qkv.shape[0] * OWN
    gated = (kc * vc).astype(BF16)
    xs[...] = gated.astype(F32).reshape(rows, BLK)
    mix = gm[...].astype(F32)
    gs[...] = (mix * conv(0).astype(BF16).astype(F32)).astype(BF16).astype(F32).reshape(rows, BLK)
    flip = (
        lax.broadcasted_iota(jnp.int32, (BLK, BLK), 0)
        + lax.broadcasted_iota(jnp.int32, (BLK, BLK), 1)
        == BLK - 1
    ).astype(F32).astype(BF16)
    xr[...] = dot(xs[...].astype(BF16), flip, 1, 0)

    eye = (
        lax.broadcasted_iota(jnp.int32, (OWN, MODES, MODES), 1)
        == lax.broadcasted_iota(jnp.int32, (OWN, MODES, MODES), 2)
    )

    def columns(ref):
        own = ref[pl.ds(pl.multiple_of(first, OWN), OWN), :]
        spread = jnp.where(eye, jnp.broadcast_to(own[:, None, :], eye.shape), 0.0)
        return jnp.sum(spread, axis=2, keepdims=True)

    shape3 = (OWN, MODES, BLK)
    time = lax.broadcasted_iota(jnp.int32, shape3, 2).astype(F32)
    weight = jnp.broadcast_to(columns(res), shape3)
    rate = jnp.exp(jnp.broadcast_to(columns(ld), shape3))
    near = jnp.exp(-rate * time)
    ahead = jnp.exp(-rate * (time + 1.0))
    back = jnp.exp(-rate * (BLK - 1.0 - time))
    taps = jnp.sum(weight * near, axis=1)
    t_ahead = (time + 1.0) * ahead
    t_back = (BLK - 1.0 - time) * back
    w_ahead = weight * ahead
    w_back = weight * back

    row2 = lax.broadcasted_iota(jnp.int32, (BLK, BLK), 0)
    lane2 = lax.broadcasted_iota(jnp.int32, (BLK, BLK), 1)
    blocks = qkv.shape[0]
    fill = jnp.zeros((BLK - blocks, BLK), F32)
    for c in range(OWN):
        own = pl.ds(c, blocks, stride=OWN)
        x = xs[own, :]
        g = gs[own, :]
        xb, gb = x.astype(BF16), g.astype(BF16)
        spread = pltpu.roll(
            jnp.broadcast_to(taps[c : c + 1], (BLK, BLK)), 0, 1, stride=1, stride_axis=0
        )
        toeplitz = jnp.where(lane2 >= row2, spread, 0.0).astype(BF16)
        here = pl.ds(c * blocks, blocks)
        fs[here, :] = dot(xb, toeplitz, 1, 0)
        gg[here, :] = dot(gb, toeplitz, 1, 1)
        pair = dot(xr[own, :].astype(BF16), gb, 0, 0)
        turned = pltpu.roll(pair, 1, 1, stride=1, stride_axis=0)
        cd[pl.ds(c, 1), :] = jnp.sum(jnp.where(lane2 <= row2, turned, 0.0), axis=0, keepdims=True)
        xw = jnp.concatenate([x, fill], axis=0).astype(BF16)
        gw = jnp.concatenate([g, fill], axis=0).astype(BF16)
        left = jnp.concatenate([*halves(back[c]), *halves(t_back[c])], axis=0)
        right = jnp.concatenate([*halves(ahead[c]), *halves(t_ahead[c])], axis=0)
        up[c] = dot(left, xw, 1, 1)
        vp[c] = dot(right, gw, 1, 1)

    n = MODES
    s0, s1 = up[:, 0:n] + up[:, n : 2 * n], up[:, 2 * n : 3 * n] + up[:, 3 * n : 4 * n]
    t0, t1 = vp[:, 0:n] + vp[:, n : 2 * n], vp[:, 2 * n : 3 * n] + vp[:, 3 * n : 4 * n]
    rest = t0
    for k in (1, 2, 4, 8, 16):
        fall = jnp.exp(-rate * float(BLK * k))
        s0_k = pltpu.roll(s0, k, 2)
        s1 = s1 + fall * (pltpu.roll(s1, k, 2) + float(BLK * k) * s0_k)
        s0 = s0 + fall * s0_k
        rest = rest + fall * pltpu.roll(rest, BLK - k, 2)
    state, d_state = pltpu.roll(s0, 1, 2), pltpu.roll(s1, 1, 2)
    rest = pltpu.roll(rest, BLK - 1, 2)
    corr = cd[...][:, None, :] * near
    by_res = jnp.sum(corr + t0 * state, axis=2, keepdims=True)
    by_rate = jnp.sum(corr * time + t1 * state + t0 * d_state, axis=2, keepdims=True)
    by_log = -by_rate * weight * rate
    lane3 = lax.broadcasted_iota(jnp.int32, shape3, 2)
    mode3 = lax.broadcasted_iota(jnp.int32, shape3, 1)
    tiny = jnp.sum(
        jnp.where(lane3 == 16 + mode3, by_res, jnp.where(lane3 == 32 + mode3, by_log, 0.0)), axis=1
    )

    for c in range(OWN):
        own = pl.ds(c, blocks, stride=OWN)
        here = pl.ds(c * blocks, blocks)

        def joined(states, table):
            sh, sl = halves(states)
            th, tl = halves(table)
            a = jnp.concatenate([sh, sh, sl], axis=0)
            b = jnp.concatenate([th, tl, th], axis=0)
            return dot(a, b, 0, 0)[:blocks]

        xs[own, :] = fs[here, :] + joined(state[c], w_ahead[c])
        gs[own, :] = gg[here, :] + joined(rest[c], w_back[c])

    shape = (blocks, OWN, BLK)
    grad_gated = gs[...].reshape(shape)
    grads = (mix * xs[...].reshape(shape), grad_gated * vc, grad_gated * kc)
    lane = lax.broadcasted_iota(jnp.int32, (OWN, BLK), 1)
    for s in range(3):
        out[:, s] = sum(cols[s][j] * sooner(grads[s], j) for j in range(TAPS)).astype(BF16)
        for j in range(TAPS):
            total = jnp.sum(jnp.sum(grads[s] * later(streams[s], j), axis=0), axis=1, keepdims=True)
            tiny = jnp.where(lane == s * TAPS + j, total, tiny)
    small[...] = tiny


def mixer(qkv, gm, short_weights, residues, log_decay):
    blocks = qkv.shape[0]
    rows = blocks * OWN
    return pl.pallas_call(
        mixer_kernel,
        out_shape=(
            jax.ShapeDtypeStruct((blocks, 3, OWN, BLK), BF16),
            jax.ShapeDtypeStruct((OWN, BLK), F32),
        ),
        in_specs=[full()] * 5,
        out_specs=(full(), full()),
        scratch_shapes=[pltpu.VMEM((rows, BLK), F32)] * 5
        + [pltpu.VMEM((OWN, 4 * MODES, BLK), F32)] * 2
        + [pltpu.VMEM((OWN, BLK), F32)],
        compiler_params=pltpu.CompilerParams(vmem_limit_bytes=48 * 1024 * 1024),
        name="mixer",
    )(qkv, gm, short_weights, residues, log_decay)


def gather_kernel(q, k, v, w, g, qkv_out, gm_out, slab, inb, wbuf, gst, xbuf, pout, pin,
                  qs, qr, gss, gsr, ws, wr, ls, lr, rs, rr, ps, pr):
    p = lax.axis_index("pos")
    c = lax.axis_index("chan")
    h, x, core = p // ROW, (p // CORES) % XN, p % CORES
    l, z = c // ZN, c % ZN
    other = (1 - l) * ZN + z
    up, down = l * ZN + (z + 1) % ZN, l * ZN + (z + ZN - 1) % ZN
    sibling = p + 1 - 2 * core

    barrier = pltpu.get_barrier_semaphore()

    @pl.loop(1, POS)
    def _(i):
        pl.semaphore_signal(barrier, 1, device_id={"pos": (p + i) % POS}, device_id_type=MESH)

    for d in (other, up, down):
        pl.semaphore_signal(barrier, 1, device_id={"chan": d}, device_id_type=MESH)

    wide = g[...].astype(F32)
    part = wide.shape[1] // YH
    for i in range(YH):
        at = i * part
        gst[i] = jnp.concatenate(
            [wide[:, at : at + part // 2], wide[:, at + part // 2 : at + part]], axis=0
        ).astype(BF16)
    pl.semaphore_wait(barrier, POS - 1 + 3)

    first = []
    for i in range(1, YH):
        to = (h + i) % YH
        first.append(remote(gst.at[to], xbuf.at[c, h], gss.at[i - 1], gsr.at[i - 1],
                            pos=to * ROW + x * CORES + core))
        first[-1].start()
    mine = x * CORES + core
    cols = w.shape[1]

    def wcols(slot):
        return wbuf.at[:, pl.ds(pl.multiple_of(slot * cols, cols), cols)]

    weights = []
    for i in (1, 3, 2):
        to = h * ROW + ((x + i) % XN) * CORES + core
        weights.append(remote(w, wcols(mine), ws.at[i - 1], wr.at[i - 1], pos=to))
        weights[-1].start()
    share = remote(w, wcols(mine), ws.at[3], wr.at[3], pos=sibling)
    share.start()
    xbuf[c, h] = gst[h]

    for s, ref in enumerate((q, k, v)):
        slab[:, s] = ref[...].astype(F32).T.astype(BF16).reshape(POS, OWN, BLK)

    for i, copy in enumerate(first):
        copy.wait_recv()
    across = remote(xbuf.at[c], xbuf.at[c], ls, lr, chan=other)
    across.start()

    def ring(way, sel, step):
        chip = (z - (step - 1) + ZN) % ZN if way == 0 else (z + step - 1) % ZN
        slot = (l if sel == 0 else 1 - l) * ZN + chip
        sem = (way * 2 + sel) * 4 + step - 1
        return remote(xbuf.at[slot], xbuf.at[slot], rs.at[sem], rr.at[sem],
                      chan=up if way == 0 else down)

    hops = []

    def send(way, sel, step):
        hops.append(ring(way, sel, step))
        hops[-1].start()

    send(0, 0, 1)
    send(1, 0, 1)

    @pl.loop(1, POS)
    def _(i):
        to = (p + i) % POS
        remote(slab.at[to], inb.at[p], qs.at[i], qr.at[i], pos=to).start()

    inb[p] = slab[p]
    wcols(mine)[...] = w[...]

    across.wait_recv()
    send(0, 1, 1)
    send(1, 1, 1)

    shared = []

    def share_weights(i):
        slot = ((x + XN - i) % XN) * CORES + core
        remote(w, wcols(slot), ws.at[i - 1], wr.at[i - 1], pos=sibling).wait_recv()
        shared.append(remote(wcols(slot), wcols(slot), ws.at[3 + i], wr.at[3 + i], pos=sibling))
        shared[-1].start()

    for step in range(1, ZN // 2 + 1):
        for sel in (0, 1):
            for way in (0, 1):
                if step == ZN // 2 and way != sel:
                    continue
                ring(way, sel, step).wait_recv()
                if step + 1 < ZN // 2 or (step + 1 == ZN // 2 and way == sel):
                    send(way, sel, step + 1)
        if step == 1:
            share_weights(1)
            share_weights(3)
        if step == 2:
            share_weights(2)
    share.wait_recv()
    for copy in shared:
        copy.wait_recv()

    half = xbuf.shape[3]
    for i in range(0, YH, 2):
        tiles = []
        for j in (i, i + 1):
            both = xbuf[:, j].astype(F32).reshape(CHAN, 2, 8, half)
            tiles.append(
                jnp.concatenate([both[:, 0].reshape(BLK, half), both[:, 1].reshape(BLK, half)], axis=1)
            )
        rows = jnp.concatenate(tiles, axis=0).astype(BF16)
        part = lax.dot_general(
            wbuf[...], rows, (((1,), (1,)), ((), ())), preferred_element_type=F32
        ).astype(BF16)
        pout[:, i] = part[:, :BLK].reshape(POS, OWN, BLK)
        pout[:, i + 1] = part[:, BLK:].reshape(POS, OWN, BLK)

    @pl.loop(1, POS)
    def _(i):
        to = (p + i) % POS
        remote(pout.at[to], pin.at[p], ps.at[i], pr.at[i], pos=to).start()

    pin[p] = pout[p]

    @pl.loop(1, POS)
    def _(i):
        at = (p + POS - i) % POS
        remote(slab.at[at], inb.at[at], qs.at[i], qr.at[i], pos=at).wait()

    qkv_out[...] = inb[...]

    @pl.loop(1, POS)
    def _(i):
        at = (p + POS - i) % POS
        remote(pout.at[at], pin.at[at], ps.at[i], pr.at[i], pos=at).wait()

    for i in range(YH):
        total = sum(pin[pl.ds(j * ROW, ROW), i].astype(F32) for j in range(YH))
        gm_out[pl.ds(i * ROW, ROW)] = total.astype(BF16)

    for copy in first + weights + [share, across] + hops + shared:
        copy.wait_send()


def gather(q, k, v, w, g):
    chans, cols = w.shape
    dma = pltpu.SemaphoreType.DMA
    half = g.shape[1] // YH // 2
    return pl.pallas_call(
        gather_kernel,
        out_shape=(
            jax.ShapeDtypeStruct((POS, 3, OWN, BLK), BF16),
            jax.ShapeDtypeStruct((POS, OWN, BLK), BF16),
        ),
        in_specs=[full()] * 5,
        out_specs=(full(), full()),
        scratch_shapes=[
            pltpu.VMEM((POS, 3, OWN, BLK), BF16),
            pltpu.VMEM((POS, 3, OWN, BLK), BF16),
            pltpu.VMEM((chans, ROW * cols), BF16),
            pltpu.VMEM((YH, 16, half), BF16),
            pltpu.VMEM((CHAN, YH, 16, half), BF16),
            pltpu.VMEM((POS, YH, OWN, BLK), BF16),
            pltpu.VMEM((POS, YH, OWN, BLK), BF16),
            dma((POS,)), dma((POS,)),
            dma((YH - 1,)), dma((YH - 1,)),
            dma((7,)), dma((7,)),
            dma, dma,
            dma((16,)), dma((16,)),
            dma((POS,)), dma((POS,)),
        ],
        compiler_params=pltpu.CompilerParams(
            collective_id=0, has_side_effects=True, vmem_limit_bytes=48 * 1024 * 1024
        ),
        name="gather",
    )(q, k, v, w, g)


def spread_kernel(gin, small, gout, sout, gb, sb, gs, gr, ss, sr):
    p = lax.axis_index("pos")
    barrier = pltpu.get_barrier_semaphore()

    @pl.loop(1, POS)
    def _(i):
        pl.semaphore_signal(barrier, 1, device_id={"pos": (p + i) % POS}, device_id_type=MESH)

    pl.semaphore_wait(barrier, POS - 1)

    @pl.loop(1, POS)
    def _(i):
        to = (p + i) % POS
        remote(gin.at[to], gb.at[p], gs.at[i], gr.at[i], pos=to).start()
        remote(small, sb.at[p], ss.at[i], sr.at[i], pos=to).start()

    gb[p] = gin[p]
    sb[p] = small[...]

    @pl.loop(1, POS)
    def _(i):
        at = (p + POS - i) % POS
        remote(gin.at[at], gb.at[at], gs.at[i], gr.at[i], pos=at).wait()
        remote(small, sb.at[at], ss.at[i], sr.at[i], pos=at).wait()

    gout[...] = gb[...]
    sout[...] = sb[...]


def spread(grads, small):
    dma = pltpu.SemaphoreType.DMA
    return pl.pallas_call(
        spread_kernel,
        out_shape=(
            jax.ShapeDtypeStruct((POS, 3, OWN, BLK), BF16),
            jax.ShapeDtypeStruct((POS, OWN, BLK), F32),
        ),
        in_specs=[full()] * 2,
        out_specs=(full(), full()),
        scratch_shapes=[
            pltpu.VMEM((POS, 3, OWN, BLK), BF16),
            pltpu.VMEM((POS, OWN, BLK), F32),
            dma((POS,)), dma((POS,)), dma((POS,)), dma((POS,)),
        ],
        compiler_params=pltpu.CompilerParams(
            collective_id=1, has_side_effects=True, vmem_limit_bytes=48 * 1024 * 1024
        ),
        name="spread",
    )(grads, small)


def finish_kernel(gin, small, q, k, v, short, res, dec):
    chans = POS * OWN
    for s, ref in enumerate((q, k, v)):
        ref[...] = gin[:, s].astype(F32).reshape(chans, BLK).T.astype(BF16)
    tiny = small[...].reshape(chans, BLK)
    res[...] = tiny[:, 16:32]
    dec[...] = tiny[:, 32:48]
    turned = tiny.T
    for s in range(3):
        short[s] = turned[s * TAPS : (s + 1) * TAPS]


def finish(grads, small):
    chans = POS * OWN
    stream = jax.ShapeDtypeStruct((BLK, chans), BF16)
    mode = jax.ShapeDtypeStruct((chans, MODES), F32)
    return pl.pallas_call(
        finish_kernel,
        out_shape=(stream, stream, stream, jax.ShapeDtypeStruct((3, TAPS, chans), F32), mode, mode),
        in_specs=[full()] * 2,
        out_specs=(full(),) * 6,
        compiler_params=pltpu.CompilerParams(vmem_limit_bytes=48 * 1024 * 1024),
        name="finish",
    )(grads, small)


def local(q_in, k_in, v_in, short_weights, residues, log_decay, out_weight, grad_out):
    qkv, gm = gather(q_in, k_in, v_in, out_weight, grad_out)
    grads, small = mixer(qkv, gm, short_weights, residues, log_decay)
    return finish(*spread(grads, small))


def solution(mesh):
    in_specs = (
        P("pos", "chan"),
        P("pos", "chan"),
        P("pos", "chan"),
        P(None, None, "chan"),
        P("chan", None),
        P("chan", None),
        P("chan", "pos"),
        P(("pos", "chan"), None),
    )
    out_specs = (
        P("pos", "chan"),
        P("pos", "chan"),
        P("pos", "chan"),
        P(None, None, "chan"),
        P("chan", None),
        P("chan", None),
    )
    return jax.shard_map(local, mesh=mesh, in_specs=in_specs, out_specs=out_specs, check_vma=False)
```

time: 499 us -> 99 us (0.20); the launches traced: 489 us -> 97 us
  waiting for transfers between devices: 157 us -> 0 us
  blocking collectives: 135 us -> 0 us
  Pallas kernels: 0 us -> 91.1 us
  matrix products: 57.3 us -> 0 us
  local copies, waits for them, and re-layouts: 53.1 us -> 5.12 us
  starting transfers between devices: 37.1 us -> 0 us
  other arithmetic: 34.1 us -> 0 us
  between operations: 14.9 us -> 0.73 us
    psum x1 -> x0, blocking collectives: 135 us -> none  [local(): lax.psum(short_part.astype(jnp.bfloat16), 'pos').astype(jnp.float32)]
    all_gather x2 -> x0, waiting for transfers between devices: 131 us -> none  [the longest x1 100 us: local(): lax.all_gather(out_weight, 'pos', axis=1, tiled=True)]
    pallas_call x0 -> x4, Pallas kernels: none -> 91.1 us  [the longest x1 63.8 us: gather(): pl.pallas_call(gather_kernel, out_shape=(jax.ShapeDtypeStruct((POS, 3, OW...]
    dot_general x40 -> x0, matrix products: 57.3 us -> none  [the longest x1 9.03 us: mode_sums(): plain = jnp.einsum('cab,cnb->cna', pieces, near, precision=HIGHEST)]
    all_to_all x4 -> x0, starting transfers between devices: 30.2 us -> none  [the longest x1 9.94 us: local(): lax.all_to_all(gated[None], 'pos', split_axis=1, concat_axis=2, tiled=True)]
    unnamed x39 -> x16, local copies, waits for them, and re-layouts: 31.2 us -> 3.68 us
    all_to_all x4 -> x0, waiting for transfers between devices: 24.7 us -> none  [the longest x1 11.1 us: local(): lax.all_to_all(gated[None], 'pos', split_axis=1, concat_axis=2, tiled=True)]
    unnamed x3 -> x0, other arithmetic: 23.8 us -> none
  transfers between devices with their start and end apart: 8 -> 0, of which waited for: 5 -> 0; matrix products, arithmetic and copies ran while one was open for 13% -> 0% of each run, Pallas kernels for 0% -> 0%
where the time goes in v1:
time: 99 us; the launch traced here: 97 us
  Pallas kernels  91.1 us (92%)
  local copies, waits for them, and re-layouts  5.12 us (5%)
    pallas_call x1, Pallas kernels, gather(): pl.pallas_call(gather_kernel, out_shape=(jax.ShapeDtypeStruct((POS, 3, OW...  63.8 us
    pallas_call x1, Pallas kernels, spread(): pl.pallas_call(spread_kernel, out_shape=(jax.ShapeDtypeStruct((POS, 3, OW...  21.8 us
    pallas_call x1, Pallas kernels, mixer(): pl.pallas_call(mixer_kernel, out_shape=(jax.ShapeDtypeStruct((blocks, 3,...  4.62 us
    unnamed x16, local copies, waits for them, and re-layouts  3.68 us

profile of v1, /device:TPU:1, one launch (start us, length us, event | category | flops | bytes accessed | tf_op | source)
XLA Modules:
  0.0 97.0 jit_solution(13980216860993264658)
XLA Ops:
  0.6 0.0 copy-start
  0.6 0.0 copy-start.6
  0.7 0.9 copy.14.res
  1.6 0.0 copy-done.6
  1.6 0.0 copy-start.1
  1.6 0.0 copy-start.2
  1.6 0.1 copy.15.ld
  1.8 0.0 copy-done
  1.8 0.7 copy-done.1
  2.5 0.1 copy-done.2
  2.6 0.0 copy-start.3
  2.6 0.9 copy-done.3
  3.5 0.0 copy-start.4
  3.5 0.9 copy-done.4
  4.4 0.0 copy-start.5
  4.4 63.8 %gather.1 = (bf16[32,3,16,128]{3,2,1,0:T(8,128)(2,1)S(1)}, bf16[32,16,128]{2,1,0:T(8,128)(2,1)S(1)}) custom-call(bf16[128,512]{1,0:T(8,128)(2,1)S(1)} %copy-done.1, bf16[128,512]{1,0:T(8,128)(2,1)S(1)} %copy-done.2, bf16[128,512]{1,0:T(8,128)(2,1)S(1)} %copy-done.3, bf16[512,256]{1,0:T(8,128)(2,1)S(1)} %copy-done, bf16[8,8192]{1,0:T(8,128)(2,1)S(1)} %copy-done.4), custom_call_target="tpu_custom_call" | custom-call | tf_op jit(solution)/shard_map/gather/pallas_call | solution.py:367
  68.2 0.0 copy-done.5
  68.2 4.6 %mixer.1 = (bf16[32,3,16,128]{3,2,1,0:T(8,128)(2,1)S(1)}, f32[16,128]{1,0:T(8,128)S(1)}) custom-call(bf16[32,3,16,128]{3,2,1,0:T(8,128)(2,1)S(1)} %get-tuple-element.12.qkv, bf16[32,16,128]{2,1,0:T(8,128)(2,1)S(1)} %get-tuple-element.13.gm, f32[3,3,512]{2,1,0:T(4,128)S(1)} %copy-done.5, f32[512,16]{1,0:T(8,128)S(1)} %copy.14.res, f32[512,16]{1,0:T(8,128)S(1)} %copy.15.ld), custom_call_target="tpu_custom_call" | custom-call | tf_op jit(solution)/shard_map/mixer/pallas_call | solution.py:195
  72.8 21.8 %spread.1 = (bf16[32,3,16,128]{3,2,1,0:T(8,128)(2,1)S(1)}, f32[32,16,128]{2,1,0:T(8,128)S(1)}) custom-call(bf16[32,3,16,128]{3,2,1,0:T(8,128)(2,1)S(1)} %get-tuple-element.14.gin, f32[16,128]{1,0:T(8,128)S(1)} %get-tuple-element.15.small), custom_call_target="tpu_custom_call" | custom-call | tf_op jit(solution)/shard_map/spread/pallas_call | solution.py:428
  94.6 1.0 %finish.1 = (bf16[128,512]{1,0:T(8,128)(2,1)}, bf16[128,512]{1,0:T(8,128)(2,1)}, bf16[128,512]{1,0:T(8,128)(2,1)}, f32[3,3,512]{2,1,0:T(4,128)}, f32[512,16]{1,0:T(8,128)S(1)}, /*index=5*/f32[512,16]{1,0:T(8,128)S(1)}) custom-call(bf16[32,3,16,128]{3,2,1,0:T(8,128)(2,1)S(1)} %get-tuple-element.16.gin, f32[32,16,128]{2,1,0:T(8,128)S(1)} %get-tuple-element.17.small), custom_call_target="tpu_custom_call" | custom-call | tf_op jit(solution)/shard_map/finish/pallas_call | solution.py:464
  95.6 0.7 copy.16
  96.3 0.7 copy.17
Async XLA Ops:
  0.6 1.1 %copy-start = (bf16[512,256]{1,0:T(8,128)(2,1)S(1)}, bf16[512,256]{1,0:T(8,128)(2,1)}, u32[]{:S(2)}) copy-start(bf16[512,256]{1,0:T(8,128)(2,1)} %w.1) | copy-start | bytes 786436
  0.6 0.9 copy-start.6
  1.6 0.9 copy-start.1
  1.6 1.0 copy-start.2
  2.6 0.9 copy-start.3
  3.5 0.9 copy-start.4
  4.4 63.8 %copy-start.5 = (f32[3,3,512]{2,1,0:T(4,128)S(1)}, f32[3,3,512]{2,1,0:T(4,128)}, u32[]{:S(2)}) copy-start(f32[3,3,512]{2,1,0:T(4,128)} %sw.1) | copy-start | bytes 55300

commit v2 on v1

v2 whole, which is shorter than its diff:
```python
import functools

import jax
import jax.numpy as jnp
from jax import lax
from jax.experimental import pallas as pl
from jax.experimental.pallas import tpu as pltpu
from jax.sharding import PartitionSpec as P

F32 = jnp.float32
BF16 = jnp.bfloat16
MESH = pl.DeviceIdType.MESH

YH, XN, CORES = 4, 4, 2
YL, ZN = 2, 8
POS = YH * XN * CORES
CHAN = YL * ZN
ROW = XN * CORES
BLK = 128
OWN = 16
MODES = 16
TAPS = 3


def remote(src, dst, send, recv, **device):
    return pltpu.make_async_remote_copy(
        src_ref=src, dst_ref=dst, send_sem=send, recv_sem=recv,
        device_id=device, device_id_type=MESH,
    )


def full(memory=pltpu.VMEM):
    return pl.BlockSpec(memory_space=memory)


def later(x, j):
    if j == 0:
        return x
    lane = lax.broadcasted_iota(jnp.int32, x.shape, 2)
    turned = pltpu.roll(x, j, 2)
    before = jnp.concatenate([jnp.zeros_like(turned[:1]), turned[:-1]], axis=0)
    return jnp.where(lane < j, before, turned)


def sooner(x, j):
    if j == 0:
        return x
    lane = lax.broadcasted_iota(jnp.int32, x.shape, 2)
    turned = pltpu.roll(x, BLK - j, 2)
    after = jnp.concatenate([turned[1:], jnp.zeros_like(turned[:1])], axis=0)
    return jnp.where(lane >= BLK - j, after, turned)


def halves(x):
    high = x.astype(BF16)
    return high, (x - high.astype(F32)).astype(BF16)


def dot(a, b, da, db):
    return lax.dot_general(a, b, (((da,), (db,)), ((), ())), preferred_element_type=F32)


def joined(states, table):
    sh, sl = halves(states)
    th, tl = halves(table)
    return dot(jnp.concatenate([sh, sh, sl], axis=0), jnp.concatenate([th, tl, th], axis=0), 0, 0)


ORDER = [(0, 0, 0), (1, 0, 0)]
for hop in range(1, ZN // 2):
    ORDER += [(0, 0, hop), (0, 1, hop), (1, 0, hop), (1, 1, hop)]
ORDER += [(0, 0, ZN // 2), (1, 1, ZN // 2)]
SLOT = {key: i for i, key in enumerate(ORDER)}
GROUP = 4
GROUPS = CHAN // GROUP


def mixer_kernel(
    q, k, v, sw, res, ld, w, g, gq_out, gkv_out, small_out,
    qkv, gbuf, swv, resv, ldv, slab, inb, wbuf, gst, xbuf, pout, pin, perm,
    xs, xr, gs, fs, gg, up, vp, cd, toep, gqs, gkvs, gqb, gkvb, smalls, smallb,
    local, qs, qr, gss, gsr, ws, wr, ls, lr, rs, rr, ps, pr, os, orr,
):
    p = lax.axis_index("pos")
    c = lax.axis_index("chan")
    h, x, core = p // ROW, (p // CORES) % XN, p % CORES
    l, z = c // ZN, c % ZN
    other = (1 - l) * ZN + z
    up_z, down_z = l * ZN + (z + 1) % ZN, l * ZN + (z + ZN - 1) % ZN
    sibling = p + 1 - 2 * core
    mine = x * CORES + core
    cols = w.shape[1]
    first_chan = p * OWN

    def wcols(slot):
        return wbuf.at[:, pl.ds(pl.multiple_of(slot * cols, cols), cols)]

    loads = [
        pltpu.make_async_copy(src, dst, local.at[i])
        for i, (src, dst) in enumerate(
            [(g, gbuf), (w, wcols(mine)), (q, qkv.at[0]), (k, qkv.at[1]), (v, qkv.at[2]),
             (sw, swv), (res, resv), (ld, ldv)]
        )
    ]
    for copy in loads:
        copy.start()

    barrier = pltpu.get_barrier_semaphore()

    @pl.loop(1, POS)
    def _(i):
        pl.semaphore_signal(barrier, 1, device_id={"pos": (p + i) % POS}, device_id_type=MESH)

    for d in (other, up_z, down_z):
        pl.semaphore_signal(barrier, 1, device_id={"chan": d}, device_id_type=MESH)

    loads[0].wait()
    wide = gbuf[...].astype(F32)
    part = wide.shape[1] // YH
    for i in range(YH):
        at = i * part
        gst[i] = jnp.concatenate(
            [wide[:, at : at + part // 2], wide[:, at + part // 2 : at + part]], axis=0
        ).astype(BF16)
    loads[1].wait()
    pl.semaphore_wait(barrier, POS - 1 + 3)

    first = []
    for i in range(1, YH):
        to = (h + i) % YH
        first.append(remote(gst.at[to], xbuf.at[0, h], gss.at[i - 1], gsr.at[i - 1],
                            pos=to * ROW + x * CORES + core))
        first[-1].start()
    weights = []
    for i in (1, 3, 2):
        to = h * ROW + ((x + i) % XN) * CORES + core
        weights.append(remote(wcols(mine), wcols(mine), ws.at[i - 1], wr.at[i - 1], pos=to))
        weights[-1].start()
    share = remote(wcols(mine), wcols(mine), ws.at[3], wr.at[3], pos=sibling)
    share.start()
    xbuf[0, h] = gst[h]

    for s in range(3):
        loads[2 + s].wait()
        slab[:, s] = qkv[s].astype(F32).T.astype(BF16).reshape(POS, OWN, BLK)

    for copy in first:
        copy.wait_recv()
    across = remote(xbuf.at[0], xbuf.at[1], ls, lr, chan=other)
    across.start()

    def ring(way, sel, hop):
        source = (sel, way if hop > 1 else 0, hop - 1)
        to = SLOT[(sel, way, hop)]
        return remote(xbuf.at[SLOT[source]], xbuf.at[to], rs.at[to], rr.at[to],
                      chan=up_z if way == 0 else down_z)

    hops = []

    def send(way, sel, hop):
        hops.append(ring(way, sel, hop))
        hops[-1].start()

    send(0, 0, 1)
    send(1, 0, 1)

    @pl.loop(1, POS)
    def _(i):
        to = (p + i) % POS
        remote(slab.at[to], inb.at[p], qs, qr, pos=to).start()

    inb[p] = slab[p]

    across.wait_recv()
    send(0, 1, 1)
    send(1, 1, 1)

    shared = []

    def share_weights(i):
        slot = ((x + XN - i) % XN) * CORES + core
        remote(wcols(slot), wcols(slot), ws.at[i - 1], wr.at[i - 1], pos=sibling).wait_recv()
        shared.append(remote(wcols(slot), wcols(slot), ws.at[3 + i], wr.at[3 + i], pos=sibling))
        shared[-1].start()

    def arrive(sel, hop):
        for way in (0, 1):
            if (sel, way, hop) in SLOT:
                ring(way, sel, hop).wait_recv()
                if (sel, way, hop + 1) in SLOT:
                    send(way, sel, hop + 1)

    half = xbuf.shape[3]
    rest_slots = pl.ds(0, POS - 1)

    def project(group):
        both = xbuf[pl.ds(group * GROUP, GROUP)].astype(F32).reshape(GROUP * YH, 2, 8, half)
        rows = jnp.concatenate(
            [both[:, 0].reshape(BLK, half), both[:, 1].reshape(BLK, half)], axis=1
        ).astype(BF16)
        pout[group] = dot(wbuf[...], rows, 1, 1).astype(BF16).reshape(POS, OWN, BLK)

        @pl.loop(1, POS)
        def _(i):
            to = (p + i) % POS
            remote(pout.at[group, to], pin.at[group, p], ps.at[group], pr.at[group], pos=to).start()

        pin[group, p] = pout[group, p]

    arrive(0, 1)
    share_weights(1)
    share_weights(3)
    arrive(1, 1)
    share_weights(2)
    arrive(0, 2)
    share.wait_recv()
    for copy in shared:
        copy.wait_recv()
    project(0)
    arrive(1, 2)
    project(1)

    for copy in loads[5:]:
        copy.wait()
    chans = swv.shape[2]
    pick = lax.broadcasted_iota(jnp.int32, (OWN, chans), 1) == (
        first_chan + lax.broadcasted_iota(jnp.int32, (OWN, chans), 0)
    )
    taps_of = [
        [
            jnp.sum(jnp.where(pick, swv[s, pl.ds(j, 1), :], 0.0), axis=1, keepdims=True)[None]
            for j in range(TAPS)
        ]
        for s in range(3)
    ]
    eye = (
        lax.broadcasted_iota(jnp.int32, (OWN, MODES, MODES), 1)
        == lax.broadcasted_iota(jnp.int32, (OWN, MODES, MODES), 2)
    )

    def columns(ref):
        own = pltpu.roll(ref[...], chans - first_chan, 1)[:, :BLK].T[:OWN]
        spread = jnp.where(eye, jnp.broadcast_to(own[:, None, :], eye.shape), 0.0)
        return jnp.sum(spread, axis=2, keepdims=True)

    shape3 = (OWN, MODES, BLK)
    time = lax.broadcasted_iota(jnp.int32, shape3, 2).astype(F32)
    weight = jnp.broadcast_to(columns(resv), shape3)
    rate = jnp.exp(jnp.broadcast_to(columns(ldv), shape3))
    near = jnp.exp(-rate * time)
    ahead = jnp.exp(-rate * (time + 1.0))
    back = jnp.exp(-rate * (BLK - 1.0 - time))
    taps = jnp.sum(weight * near, axis=1)
    t_ahead = (time + 1.0) * ahead
    t_back = (BLK - 1.0 - time) * back
    w_ahead = weight * ahead
    w_back = weight * back

    arrive(0, 3)
    remote(slab.at[rest_slots], inb.at[rest_slots], qs, qr, pos=sibling).wait()
    blocks = POS
    rows = blocks * OWN
    shape = (blocks, OWN, BLK)

    def stream(s):
        return inb[:, s].astype(F32)

    def conv(s):
        values = stream(s)
        return sum(taps_of[s][j] * later(values, j) for j in range(TAPS))

    xs[...] = (conv(1) * conv(2)).astype(BF16).astype(F32).reshape(rows, BLK)
    row2 = lax.broadcasted_iota(jnp.int32, (BLK, BLK), 0)
    lane2 = lax.broadcasted_iota(jnp.int32, (BLK, BLK), 1)
    flip = (row2 + lane2 == BLK - 1).astype(F32).astype(BF16)
    xr[...] = dot(xs[...].astype(BF16), flip, 1, 0)
    project(2)
    arrive(1, 3)

    fill = jnp.zeros((BLK - blocks, BLK), F32)

    def strided(i):
        return pl.ds(i, blocks, stride=OWN)

    for i in range(OWN):
        gated = xs[strided(i), :]
        turned = pltpu.roll(
            jnp.broadcast_to(taps[i : i + 1], (BLK, BLK)), 0, 1, stride=1, stride_axis=0
        )
        toep[i] = jnp.where(lane2 >= row2, turned, 0.0).astype(BF16)
        fs[pl.ds(i * blocks, blocks), :] = dot(gated.astype(BF16), toep[i], 1, 0)
        up[i] = dot(
            jnp.concatenate([*halves(back[i]), *halves(t_back[i])], axis=0),
            jnp.concatenate([gated, fill], axis=0).astype(BF16), 1, 1,
        )

    n = MODES
    s0, s1 = up[:, 0:n] + up[:, n : 2 * n], up[:, 2 * n : 3 * n] + up[:, 3 * n : 4 * n]
    falls = []
    for e in range(5):
        skip = 1 << e
        falls.append(jnp.exp(-rate * float(BLK * skip)))
        s0_k = pltpu.roll(s0, skip, 2)
        s1 = s1 + falls[e] * (pltpu.roll(s1, skip, 2) + float(BLK * skip) * s0_k)
        s0 = s0 + falls[e] * s0_k
    state, d_state = pltpu.roll(s0, 1, 2), pltpu.roll(s1, 1, 2)
    for i in range(OWN):
        xs[strided(i), :] = (
            fs[pl.ds(i * blocks, blocks), :] + joined(state[i], w_ahead[i])[:blocks]
        )

    lanes = GROUPS * BLK
    each = BLK // GROUP
    row_p = lax.broadcasted_iota(jnp.int32, (each, lanes), 0)
    lane_p = lax.broadcasted_iota(jnp.int32, (each, lanes), 1)
    for i, (sel, way, hop) in enumerate(ORDER):
        chip = (z + ZN - hop) % ZN if way == 0 else (z + hop) % ZN
        chunk = (l if sel == 0 else 1 - l) * ZN + chip
        goes = (row_p // 8) * BLK + chunk * 8 + row_p % 8
        perm[pl.ds(i * each, each), :] = (lane_p == goes).astype(F32).astype(BF16)

    for sel, way, hop in ORDER[-2:]:
        ring(way, sel, hop).wait_recv()
    project(3)

    own_rows = ROW * OWN
    tiles = []
    for i in range(GROUPS):
        remote(pout.at[i, rest_slots], pin.at[i, rest_slots], ps.at[i], pr.at[i], pos=sibling).wait()
        total = sum(pin[i, pl.ds(j * ROW, ROW)].astype(F32) for j in range(YH))
        tiles.append(total.reshape(own_rows, BLK).astype(BF16))
    ordered = dot(jnp.concatenate(tiles, axis=1), perm[...], 1, 0)
    mix = jnp.concatenate(
        [ordered[:, i * BLK : (i + 1) * BLK].reshape(ROW, OWN, BLK) for i in range(YH)], axis=0
    )

    lane = lax.broadcasted_iota(jnp.int32, (OWN, BLK), 1)
    sums = []

    def finish_stream(s, grad, ref, index):
        values = stream(s)
        total = sum(taps_of[s][j] * sooner(grad, j) for j in range(TAPS)).astype(BF16)
        if index is None:
            ref[...] = total
        else:
            ref[:, index] = total
        for j in range(TAPS):
            sums.append(
                jnp.sum(jnp.sum(grad * later(values, j), axis=0), axis=1, keepdims=True)
            )

    def give(mine_ref, all_ref, sem):
        @pl.loop(1, POS)
        def _(i):
            to = (p + i) % POS
            remote(mine_ref.at[to], all_ref.at[p], os.at[sem], orr.at[sem], pos=to).start()

        all_ref[p] = mine_ref[p]

    finish_stream(0, mix * xs[...].reshape(shape), gqs, None)
    give(gqs, gqb, 0)

    gs[...] = (mix * conv(0).astype(BF16).astype(F32)).astype(BF16).astype(F32).reshape(rows, BLK)
    for i in range(OWN):
        grad = gs[strided(i), :]
        low = grad.astype(BF16)
        gg[pl.ds(i * blocks, blocks), :] = dot(low, toep[i], 1, 1)
        vp[i] = dot(
            jnp.concatenate([*halves(ahead[i]), *halves(t_ahead[i])], axis=0),
            jnp.concatenate([grad, fill], axis=0).astype(BF16), 1, 1,
        )
    t0, t1 = vp[:, 0:n] + vp[:, n : 2 * n], vp[:, 2 * n : 3 * n] + vp[:, 3 * n : 4 * n]
    rest = t0
    for e in range(5):
        rest = rest + falls[e] * pltpu.roll(rest, BLK - (1 << e), 2)
    rest = pltpu.roll(rest, BLK - 1, 2)
    for i in range(OWN):
        pair = dot(xr[strided(i), :].astype(BF16), gs[strided(i), :].astype(BF16), 0, 0)
        turned = pltpu.roll(pair, 1, 1, stride=1, stride_axis=0)
        cd[pl.ds(i, 1), :] = jnp.sum(jnp.where(lane2 <= row2, turned, 0.0), axis=0, keepdims=True)
        xs[strided(i), :] = (
            gg[pl.ds(i * blocks, blocks), :] + joined(rest[i], w_back[i])[:blocks]
        )
    grad_gated = xs[...].reshape(shape)
    finish_stream(1, grad_gated * conv(2), gkvs, 0)
    finish_stream(2, grad_gated * conv(1), gkvs, 1)
    give(gkvs, gkvb, 1)

    corr = cd[...][:, None, :] * near
    by_res = jnp.sum(corr + t0 * state, axis=2, keepdims=True)
    by_rate = jnp.sum(corr * time + t1 * state + t0 * d_state, axis=2, keepdims=True)
    by_log = -by_rate * weight * rate
    lane3 = lax.broadcasted_iota(jnp.int32, shape3, 2)
    mode3 = lax.broadcasted_iota(jnp.int32, shape3, 1)
    tiny = jnp.sum(
        jnp.where(lane3 == 16 + mode3, by_res, jnp.where(lane3 == 32 + mode3, by_log, 0.0)), axis=1
    )
    for j, total in enumerate(sums):
        tiny = jnp.where(lane == j, total, tiny)
    smalls[...] = jnp.where(lane[:8] < BLK // 2, tiny[:8], pltpu.roll(tiny[8:], BLK // 2, 1))

    @pl.loop(1, POS)
    def _(i):
        to = (p + i) % POS
        remote(smalls, smallb.at[p], os.at[2], orr.at[2], pos=to).start()

    smallb[p] = smalls[...]

    for copy in first + weights + [share, across] + hops + shared:
        copy.wait_send()
    for sem, (ref, out) in enumerate(((gqb, gq_out), (gkvb, gkv_out), (smallb, small_out))):
        remote(ref.at[rest_slots], ref.at[rest_slots], os.at[sem], orr.at[sem], pos=sibling).wait()
        out[...] = ref[...]


def mixer(q, k, v, short_weights, residues, log_decay, w, g):
    chans, cols = w.shape
    dma = pltpu.SemaphoreType.DMA
    half = g.shape[1] // YH // 2
    rows = POS * OWN
    outs = [((POS, OWN, BLK), BF16), ((POS, 2, OWN, BLK), BF16), ((POS, 8, BLK), F32)]
    return pl.pallas_call(
        mixer_kernel,
        out_shape=tuple(jax.ShapeDtypeStruct(*o) for o in outs),
        in_specs=[full(pl.ANY)] * 8,
        out_specs=(full(),) * 3,
        scratch_shapes=[
            pltpu.VMEM((3, BLK, chans), BF16),
            pltpu.VMEM(g.shape, BF16),
            pltpu.VMEM(short_weights.shape, F32),
            pltpu.VMEM(residues.shape, F32),
            pltpu.VMEM(log_decay.shape, F32),
            pltpu.VMEM((POS, 3, OWN, BLK), BF16),
            pltpu.VMEM((POS, 3, OWN, BLK), BF16),
            pltpu.VMEM((chans, ROW * cols), BF16),
            pltpu.VMEM((YH, 16, half), BF16),
            pltpu.VMEM((CHAN, YH, 16, half), BF16),
            pltpu.VMEM((GROUPS, POS, OWN, BLK), BF16),
            pltpu.VMEM((GROUPS, POS, OWN, BLK), BF16),
            pltpu.VMEM((GROUPS * BLK, GROUPS * BLK), BF16),
        ]
        + [pltpu.VMEM((rows, BLK), F32)] * 5
        + [pltpu.VMEM((OWN, 4 * MODES, BLK), F32)] * 2
        + [pltpu.VMEM((OWN, BLK), F32), pltpu.VMEM((OWN, BLK, BLK), BF16)]
        + [pltpu.VMEM(*o) for o in (outs[0], outs[1], outs[0], outs[1])]
        + [pltpu.VMEM((8, BLK), F32), pltpu.VMEM(*outs[2])]
        + [
            dma((8,)),
            dma, dma,
            dma((YH - 1,)), dma((YH - 1,)),
            dma((7,)), dma((7,)),
            dma, dma,
            dma((CHAN,)), dma((CHAN,)),
            dma((GROUPS,)), dma((GROUPS,)),
            dma((3,)), dma((3,)),
        ],
        compiler_params=pltpu.CompilerParams(
            collective_id=0, has_side_effects=True, vmem_limit_bytes=48 * 1024 * 1024
        ),
        name="mixer",
    )(q, k, v, short_weights, residues, log_decay, w, g)


def finish_kernel(gq, gkv, small, q, k, v, short, res, dec):
    chans = POS * OWN
    q[...] = gq[...].astype(F32).reshape(chans, BLK).T.astype(BF16)
    for s, ref in enumerate((k, v)):
        ref[...] = gkv[:, s].astype(F32).reshape(chans, BLK).T.astype(BF16)
    packed = small[...]
    both = jnp.concatenate([packed, pltpu.roll(packed, BLK // 2, 2)], axis=1)
    turned = both.reshape(chans, BLK).T
    res[...] = turned[16:32]
    dec[...] = turned[32:48]
    for s in range(3):
        short[s] = turned[s * TAPS : (s + 1) * TAPS]


def finish(gq, gkv, small):
    chans = POS * OWN
    stream = jax.ShapeDtypeStruct((BLK, chans), BF16)
    mode = jax.ShapeDtypeStruct((MODES, chans), F32)
    return pl.pallas_call(
        finish_kernel,
        out_shape=(stream, stream, stream, jax.ShapeDtypeStruct((3, TAPS, chans), F32), mode, mode),
        in_specs=[full()] * 3,
        out_specs=(full(),) * 6,
        compiler_params=pltpu.CompilerParams(vmem_limit_bytes=48 * 1024 * 1024),
        name="finish",
    )(gq, gkv, small)


def local(q_in, k_in, v_in, short_weights, residues, log_decay, out_weight, grad_out):
    parts = mixer(
        q_in, k_in, v_in, short_weights, residues.T, log_decay.T, out_weight, grad_out
    )
    gq, gk, gv, short, res, dec = finish(*parts)
    return gq, gk, gv, short, res.T, dec.T


def solution(mesh):
    in_specs = (
        P("pos", "chan"),
        P("pos", "chan"),
        P("pos", "chan"),
        P(None, None, "chan"),
        P("chan", None),
        P("chan", None),
        P("chan", "pos"),
        P(("pos", "chan"), None),
    )
    out_specs = (
        P("pos", "chan"),
        P("pos", "chan"),
        P("pos", "chan"),
        P(None, None, "chan"),
        P("chan", None),
        P("chan", None),
    )
    return jax.shard_map(local, mesh=mesh, in_specs=in_specs, out_specs=out_specs, check_vma=False)
```

time: 99 us -> 85.1 us (0.86); the launches traced: 97 us -> 84.7 us
  Pallas kernels: 91.1 us -> 77.3 us
  local copies, waits for them, and re-layouts: 5.12 us -> 6.81 us
    pallas_call x3 -> x1, Pallas kernels: 90.1 us -> 76.3 us  [mixer(): pl.pallas_call(mixer_kernel, out_shape=tuple((jax.ShapeDtypeStruct(*o) fo...]
    unnamed x16, local copies, waits for them, and re-layouts: 3.68 us -> 6.81 us
    pallas_call x2 -> x0, local copies, waits for them, and re-layouts: 1.44 us -> none  [finish(): pl.pallas_call(finish_kernel, out_shape=(stream, stream, stream, jax.Shap...]
where the time goes in v2:
time: 85.1 us; the launch traced here: 84.7 us
  Pallas kernels  77.3 us (91%)
  local copies, waits for them, and re-layouts  6.81 us (8%)
    pallas_call x1, Pallas kernels, mixer(): pl.pallas_call(mixer_kernel, out_shape=tuple((jax.ShapeDtypeStruct(*o) fo...  76.3 us
    unnamed x16, local copies, waits for them, and re-layouts  6.81 us

profile of v2, /device:TPU:1, one launch (start us, length us, event | category | flops | bytes accessed | tf_op | source)
XLA Modules:
  0.0 84.7 jit_solution(1935416017919069665)
XLA Ops:
  0.6 0.0 copy-start
  0.6 0.9 %copy-done = bf16[512,256]{1,0:T(8,128)(2,1)S(1)} copy-done((bf16[512,256]{1,0:T(8,128)(2,1)S(1)}, bf16[512,256]{1,0:T(8,128)(2,1)}, u32[]{:S(2)}) %copy-start) | copy-done | bytes 262168
  1.6 0.0 copy-start.1
  1.6 0.9 %copy-done.1 = bf16[128,512]{1,0:T(8,128)(2,1)S(1)} copy-done((bf16[128,512]{1,0:T(8,128)(2,1)S(1)}, bf16[128,512]{1,0:T(8,128)(2,1)}, u32[]{:S(2)}) %copy-start.1) | copy-done | bytes 131096
  2.5 0.0 copy-start.2
  2.5 0.9 %copy-done.2 = bf16[128,512]{1,0:T(8,128)(2,1)S(1)} copy-done((bf16[128,512]{1,0:T(8,128)(2,1)S(1)}, bf16[128,512]{1,0:T(8,128)(2,1)}, u32[]{:S(2)}) %copy-start.2) | copy-done | bytes 131096
  3.4 0.0 copy-start.3
  3.4 0.9 %copy-done.3 = bf16[128,512]{1,0:T(8,128)(2,1)S(1)} copy-done((bf16[128,512]{1,0:T(8,128)(2,1)S(1)}, bf16[128,512]{1,0:T(8,128)(2,1)}, u32[]{:S(2)}) %copy-start.3) | copy-done | bytes 131096
  4.3 0.0 copy-start.4
  4.3 0.9 %copy-done.4 = bf16[8,8192]{1,0:T(8,128)(2,1)S(1)} copy-done((bf16[8,8192]{1,0:T(8,128)(2,1)S(1)}, bf16[8,8192]{1,0:T(8,128)(2,1)}, u32[]{:S(2)}) %copy-start.4) | copy-done | bytes 131096
  5.2 0.0 copy-start.5
  5.2 0.8 copy-done.5
  6.0 0.0 copy-start.6
  6.0 0.8 copy-done.6
  6.7 0.0 copy-start.7
  6.7 0.7 copy-done.7
  7.5 76.3 %mixer.1 = (bf16[32,16,128]{2,1,0:T(8,128)(2,1)S(1)}, bf16[32,2,16,128]{3,2,1,0:T(8,128)(2,1)S(1)}, f32[32,8,128]{2,1,0:T(8,128)S(1)}) custom-call(bf16[128,512]{1,0:T(8,128)(2,1)S(1)} %copy-done.1, bf16[128,512]{1,0:T(8,128)(2,1)S(1)} %copy-done.2, bf16[128,512]{1,0:T(8,128)(2,1)S(1)} %copy-done.3, f32[3,3,512]{2,1,0:T(4,128)S(1)} %copy-done.7, ...), custom_call_target="tpu_custom_call" | custom-call | tf_op jit(solution)/shard_map/mixer/pallas_call | solution.py:422
  83.8 0.9 %finish.1 = (bf16[128,512]{1,0:T(8,128)(2,1)}, bf16[128,512]{1,0:T(8,128)(2,1)}, bf16[128,512]{1,0:T(8,128)(2,1)}, f32[3,3,512]{2,1,0:T(4,128)}, f32[16,512]{1,0:T(8,128)}, /*index=5*/f32[16,512]{1,0:T(8,128)}) custom-call(bf16[32,16,128]{2,1,0:T(8,128)(2,1)S(1)} %get-tuple-element.15.gq, bf16[32,2,16,128]{3,2,1,0:T(8,128)(2,1)S(1)} %get-tuple-element.16.gkv, ...), custom_call_target="tpu_custom_call" | custom-call | tf_op jit(solution)/shard_map/finish/pallas_call | solution.py:482
Async XLA Ops:
  0.6 1.0 %copy-start = (bf16[512,256]{1,0:T(8,128)(2,1)S(1)}, bf16[512,256]{1,0:T(8,128)(2,1)}, u32[]{:S(2)}) copy-start(bf16[512,256]{1,0:T(8,128)(2,1)} %w.1) | copy-start | bytes 786436
  1.6 0.9 %copy-start.1 = (bf16[128,512]{1,0:T(8,128)(2,1)S(1)}, bf16[128,512]{1,0:T(8,128)(2,1)}, u32[]{:S(2)}) copy-start(bf16[128,512]{1,0:T(8,128)(2,1)} %q.1) | copy-start | bytes 393220
  2.5 0.9 %copy-start.2 = (bf16[128,512]{1,0:T(8,128)(2,1)S(1)}, bf16[128,512]{1,0:T(8,128)(2,1)}, u32[]{:S(2)}) copy-start(bf16[128,512]{1,0:T(8,128)(2,1)} %k.1) | copy-start | bytes 393220
  3.4 0.9 %copy-start.3 = (bf16[128,512]{1,0:T(8,128)(2,1)S(1)}, bf16[128,512]{1,0:T(8,128)(2,1)}, u32[]{:S(2)}) copy-start(bf16[128,512]{1,0:T(8,128)(2,1)} %v.1) | copy-start | bytes 393220
  4.3 0.9 %copy-start.4 = (bf16[8,8192]{1,0:T(8,128)(2,1)S(1)}, bf16[8,8192]{1,0:T(8,128)(2,1)}, u32[]{:S(2)}) copy-start(bf16[8,8192]{1,0:T(8,128)(2,1)} %g.1) | copy-start | bytes 393220
  5.2 0.8 copy-start.5
  6.0 0.8 copy-start.6
  6.7 0.7 copy-start.7

commit v3 on v2

--- a/solution.py
+++ b/solution.py
@@ -20,6 +20,7 @@
 OWN = 16
 MODES = 16
 TAPS = 3
+VMEM = 60 * 1024 * 1024
 
 
 def remote(src, dst, send, recv, **device):
@@ -71,8 +72,10 @@
     ORDER += [(0, 0, hop), (0, 1, hop), (1, 0, hop), (1, 1, hop)]
 ORDER += [(0, 0, ZN // 2), (1, 1, ZN // 2)]
 SLOT = {key: i for i, key in enumerate(ORDER)}
+NEAR = (0, 1, 3, 2)
 GROUP = 4
 GROUPS = CHAN // GROUP
+PARTS = ((0, 2), (2, 1), (3, 1))
 
 
 def mixer_kernel(
@@ -125,12 +128,38 @@
     loads[1].wait()
     pl.semaphore_wait(barrier, POS - 1 + 3)
 
+    xbuf[0, h] = gst[h]
+
+    def piece(r):
+        return (h + YH - NEAR[r]) % YH
+
+    def ring(way, sel, hop, r):
+        source = (sel, way if hop > 1 else 0, hop - 1)
+        to = SLOT[(sel, way, hop)]
+        return remote(xbuf.at[SLOT[source], piece(r)], xbuf.at[to, piece(r)],
+                      rs.at[to * YH + r], rr.at[to * YH + r],
+                      chan=up_z if way == 0 else down_z)
+
+    hops, across = [], []
+
+    def send(way, sel, hop, r):
+        hops.append(ring(way, sel, hop, r))
+        hops[-1].start()
+
+    def pass_own(r):
+        send(0, 0, 1, r)
+        send(1, 0, 1, r)
+        across.append(remote(xbuf.at[0, piece(r)], xbuf.at[1, piece(r)], ls.at[r], lr.at[r],
+                             chan=other))
+        across[-1].start()
+
     first = []
     for i in range(1, YH):
-        to = (h + i) % YH
+        to = (h + NEAR[i]) % YH
         first.append(remote(gst.at[to], xbuf.at[0, h], gss.at[i - 1], gsr.at[i - 1],
                             pos=to * ROW + x * CORES + core))
         first[-1].start()
+    pass_own(0)
     weights = []
     for i in (1, 3, 2):
         to = h * ROW + ((x + i) % XN) * CORES + core
@@ -138,31 +167,12 @@
         weights[-1].start()
     share = remote(wcols(mine), wcols(mine), ws.at[3], wr.at[3], pos=sibling)
     share.start()
-    xbuf[0, h] = gst[h]
 
     for s in range(3):
         loads[2 + s].wait()
         slab[:, s] = qkv[s].astype(F32).T.astype(BF16).reshape(POS, OWN, BLK)
-
-    for copy in first:
-        copy.wait_recv()
-    across = remote(xbuf.at[0], xbuf.at[1], ls, lr, chan=other)
-    across.start()
-
-    def ring(way, sel, hop):
-        source = (sel, way if hop > 1 else 0, hop - 1)
-        to = SLOT[(sel, way, hop)]
-        return remote(xbuf.at[SLOT[source]], xbuf.at[to], rs.at[to], rr.at[to],
-                      chan=up_z if way == 0 else down_z)
-
-    hops = []
-
-    def send(way, sel, hop):
-        hops.append(ring(way, sel, hop))
-        hops[-1].start()
-
-    send(0, 0, 1)
-    send(1, 0, 1)
+        first[s].wait_recv()
+        pass_own(s + 1)
 
     @pl.loop(1, POS)
     def _(i):
@@ -170,10 +180,6 @@
         remote(slab.at[to], inb.at[p], qs, qr, pos=to).start()
 
     inb[p] = slab[p]
-
-    across.wait_recv()
-    send(0, 1, 1)
-    send(1, 1, 1)
 
     shared = []
 
@@ -183,42 +189,40 @@
         shared.append(remote(wcols(slot), wcols(slot), ws.at[3 + i], wr.at[3 + i], pos=sibling))
         shared[-1].start()
 
-    def arrive(sel, hop):
-        for way in (0, 1):
-            if (sel, way, hop) in SLOT:
-                ring(way, sel, hop).wait_recv()
-                if (sel, way, hop + 1) in SLOT:
-                    send(way, sel, hop + 1)
+    def arrive(sel, hop, *work):
+        for r in range(YH):
+            for way in (0, 1):
+                if (sel, way, hop) in SLOT:
+                    ring(way, sel, hop, r).wait_recv()
+                    if (sel, way, hop + 1) in SLOT:
+                        send(way, sel, hop + 1, r)
+            if r < len(work):
+                work[r]()
 
     half = xbuf.shape[3]
     rest_slots = pl.ds(0, POS - 1)
 
-    def project(group):
-        both = xbuf[pl.ds(group * GROUP, GROUP)].astype(F32).reshape(GROUP * YH, 2, 8, half)
+    def product(tile):
+        both = xbuf[pl.ds(tile * GROUP, GROUP)].astype(F32).reshape(GROUP * YH, 2, 8, half)
         rows = jnp.concatenate(
             [both[:, 0].reshape(BLK, half), both[:, 1].reshape(BLK, half)], axis=1
         ).astype(BF16)
-        pout[group] = dot(wbuf[...], rows, 1, 1).astype(BF16).reshape(POS, OWN, BLK)
+        pout[:, tile] = dot(wbuf[...], rows, 1, 1).astype(BF16).reshape(POS, OWN, BLK)
+
+    def give_part(part):
+        tiles = pl.ds(*PARTS[part])
 
         @pl.loop(1, POS)
         def _(i):
             to = (p + i) % POS
-            remote(pout.at[group, to], pin.at[group, p], ps.at[group], pr.at[group], pos=to).start()
-
-        pin[group, p] = pout[group, p]
-
-    arrive(0, 1)
-    share_weights(1)
-    share_weights(3)
-    arrive(1, 1)
-    share_weights(2)
-    arrive(0, 2)
-    share.wait_recv()
-    for copy in shared:
-        copy.wait_recv()
-    project(0)
-    arrive(1, 2)
-    project(1)
+            remote(pout.at[to, tiles], pin.at[p, tiles], ps.at[part], pr.at[part], pos=to).start()
+
+        pin[p, tiles] = pout[p, tiles]
+
+    for r in range(YH):
+        across[r].wait_recv()
+        send(0, 1, 1, r)
+        send(1, 1, 1, r)
 
     for copy in loads[5:]:
         copy.wait()
@@ -256,11 +260,16 @@
     w_ahead = weight * ahead
     w_back = weight * back
 
-    arrive(0, 3)
+    arrive(0, 1)
+    arrive(1, 1)
     remote(slab.at[rest_slots], inb.at[rest_slots], qs, qr, pos=sibling).wait()
     blocks = POS
     rows = blocks * OWN
     shape = (blocks, OWN, BLK)
+    row2 = lax.broadcasted_iota(jnp.int32, (BLK, BLK), 0)
+    lane2 = lax.broadcasted_iota(jnp.int32, (BLK, BLK), 1)
+    fill = jnp.zeros((BLK - blocks, BLK), F32)
+    held = {}
 
     def stream(s):
         return inb[:, s].astype(F32)
@@ -269,66 +278,92 @@
         values = stream(s)
         return sum(taps_of[s][j] * later(values, j) for j in range(TAPS))
 
-    xs[...] = (conv(1) * conv(2)).astype(BF16).astype(F32).reshape(rows, BLK)
-    row2 = lax.broadcasted_iota(jnp.int32, (BLK, BLK), 0)
-    lane2 = lax.broadcasted_iota(jnp.int32, (BLK, BLK), 1)
-    flip = (row2 + lane2 == BLK - 1).astype(F32).astype(BF16)
-    xr[...] = dot(xs[...].astype(BF16), flip, 1, 0)
-    project(2)
-    arrive(1, 3)
-
-    fill = jnp.zeros((BLK - blocks, BLK), F32)
-
     def strided(i):
         return pl.ds(i, blocks, stride=OWN)
 
-    for i in range(OWN):
-        gated = xs[strided(i), :]
-        turned = pltpu.roll(
-            jnp.broadcast_to(taps[i : i + 1], (BLK, BLK)), 0, 1, stride=1, stride_axis=0
-        )
-        toep[i] = jnp.where(lane2 >= row2, turned, 0.0).astype(BF16)
-        fs[pl.ds(i * blocks, blocks), :] = dot(gated.astype(BF16), toep[i], 1, 0)
-        up[i] = dot(
-            jnp.concatenate([*halves(back[i]), *halves(t_back[i])], axis=0),
-            jnp.concatenate([gated, fill], axis=0).astype(BF16), 1, 1,
-        )
+    def gate():
+        xs[...] = (conv(1) * conv(2)).astype(BF16).astype(F32).reshape(rows, BLK)
+
+    def within(low, high):
+        def work():
+            for i in range(low, high):
+                gated = xs[strided(i), :]
+                turned = pltpu.roll(
+                    jnp.broadcast_to(taps[i : i + 1], (BLK, BLK)), 0, 1, stride=1, stride_axis=0
+                )
+                toep[i] = jnp.where(lane2 >= row2, turned, 0.0).astype(BF16)
+                fs[pl.ds(i * blocks, blocks), :] = dot(gated.astype(BF16), toep[i], 1, 0)
+                up[i] = dot(
+                    jnp.concatenate([*halves(back[i]), *halves(t_back[i])], axis=0),
+                    jnp.concatenate([gated, fill], axis=0).astype(BF16), 1, 1,
+                )
+        return work
 
     n = MODES
-    s0, s1 = up[:, 0:n] + up[:, n : 2 * n], up[:, 2 * n : 3 * n] + up[:, 3 * n : 4 * n]
-    falls = []
-    for e in range(5):
-        skip = 1 << e
-        falls.append(jnp.exp(-rate * float(BLK * skip)))
-        s0_k = pltpu.roll(s0, skip, 2)
-        s1 = s1 + falls[e] * (pltpu.roll(s1, skip, 2) + float(BLK * skip) * s0_k)
-        s0 = s0 + falls[e] * s0_k
-    state, d_state = pltpu.roll(s0, 1, 2), pltpu.roll(s1, 1, 2)
-    for i in range(OWN):
-        xs[strided(i), :] = (
-            fs[pl.ds(i * blocks, blocks), :] + joined(state[i], w_ahead[i])[:blocks]
-        )
+
+    def edges():
+        flip = (row2 + lane2 == BLK - 1).astype(F32).astype(BF16)
+        xr[...] = dot(xs[...].astype(BF16), flip, 1, 0)
+        s0 = up[:, 0:n] + up[:, n : 2 * n]
+        s1 = up[:, 2 * n : 3 * n] + up[:, 3 * n : 4 * n]
+        held["falls"] = falls = []
+        for e in range(5):
+            skip = 1 << e
+            falls.append(jnp.exp(-rate * float(BLK * skip)))
+            s0_k = pltpu.roll(s0, skip, 2)
+            s1 = s1 + falls[e] * (pltpu.roll(s1, skip, 2) + float(BLK * skip) * s0_k)
+            s0 = s0 + falls[e] * s0_k
+        held["state"], held["d_state"] = pltpu.roll(s0, 1, 2), pltpu.roll(s1, 1, 2)
+
+    def between(low, high):
+        def work():
+            for i in range(low, high):
+                xs[strided(i), :] = (
+                    fs[pl.ds(i * blocks, blocks), :]
+                    + joined(held["state"][i], w_ahead[i])[:blocks]
+                )
+        return work
 
     lanes = GROUPS * BLK
     each = BLK // GROUP
-    row_p = lax.broadcasted_iota(jnp.int32, (each, lanes), 0)
-    lane_p = lax.broadcasted_iota(jnp.int32, (each, lanes), 1)
-    for i, (sel, way, hop) in enumerate(ORDER):
-        chip = (z + ZN - hop) % ZN if way == 0 else (z + hop) % ZN
-        chunk = (l if sel == 0 else 1 - l) * ZN + chip
-        goes = (row_p // 8) * BLK + chunk * 8 + row_p % 8
-        perm[pl.ds(i * each, each), :] = (lane_p == goes).astype(F32).astype(BF16)
-
-    for sel, way, hop in ORDER[-2:]:
-        ring(way, sel, hop).wait_recv()
-    project(3)
+
+    def order():
+        row_p = lax.broadcasted_iota(jnp.int32, (each, lanes), 0)
+        lane_p = lax.broadcasted_iota(jnp.int32, (each, lanes), 1)
+        for i, (sel, way, hop) in enumerate(ORDER):
+            chip = (z + ZN - hop) % ZN if way == 0 else (z + hop) % ZN
+            chunk = (l if sel == 0 else 1 - l) * ZN + chip
+            goes = (row_p // 8) * BLK + chunk * 8 + row_p % 8
+            perm[pl.ds(i * each, each), :] = (lane_p == goes).astype(F32).astype(BF16)
+
+    def weights_in():
+        share.wait_recv()
+        for copy in shared:
+            copy.wait_recv()
+        product(0)
+
+    half_own = OWN // 2
+    for i in (1, 3, 2):
+        share_weights(i)
+    arrive(0, 2, gate, within(0, 5), within(5, 11), within(11, OWN))
+    arrive(1, 2, weights_in, lambda: product(1), lambda: give_part(0), edges)
+    arrive(0, 3, between(0, half_own), between(half_own, OWN), order)
+    arrive(1, 3, lambda: product(2), lambda: give_part(1))
+    for r in range(YH):
+        for sel, way, hop in ORDER[-2:]:
+            ring(way, sel, hop, r).wait_recv()
+    product(3)
+    give_part(2)
+    falls, state, d_state = held["falls"], held["state"], held["d_state"]
 
     own_rows = ROW * OWN
     tiles = []
-    for i in range(GROUPS):
-        remote(pout.at[i, rest_slots], pin.at[i, rest_slots], ps.at[i], pr.at[i], pos=sibling).wait()
-        total = sum(pin[i, pl.ds(j * ROW, ROW)].astype(F32) for j in range(YH))
-        tiles.append(total.reshape(own_rows, BLK).astype(BF16))
+    for part, (first_tile, count) in enumerate(PARTS):
+        some = (rest_slots, pl.ds(first_tile, count))
+        remote(pout.at[some], pin.at[some], ps.at[part], pr.at[part], pos=sibling).wait()
+        for i in range(first_tile, first_tile + count):
+            total = sum(pin[pl.ds(j * ROW, ROW), i].astype(F32) for j in range(YH))
+            tiles.append(total.reshape(own_rows, BLK).astype(BF16))
     ordered = dot(jnp.concatenate(tiles, axis=1), perm[...], 1, 0)
     mix = jnp.concatenate(
         [ordered[:, i * BLK : (i + 1) * BLK].reshape(ROW, OWN, BLK) for i in range(YH)], axis=0
@@ -345,9 +380,7 @@
         else:
             ref[:, index] = total
         for j in range(TAPS):
-            sums.append(
-                jnp.sum(jnp.sum(grad * later(values, j), axis=0), axis=1, keepdims=True)
-            )
+            sums.append(jnp.sum(grad * later(values, j), axis=0))
 
     def give(mine_ref, all_ref, sem):
         @pl.loop(1, POS)
@@ -375,9 +408,6 @@
         rest = rest + falls[e] * pltpu.roll(rest, BLK - (1 << e), 2)
     rest = pltpu.roll(rest, BLK - 1, 2)
     for i in range(OWN):
-        pair = dot(xr[strided(i), :].astype(BF16), gs[strided(i), :].astype(BF16), 0, 0)
-        turned = pltpu.roll(pair, 1, 1, stride=1, stride_axis=0)
-        cd[pl.ds(i, 1), :] = jnp.sum(jnp.where(lane2 <= row2, turned, 0.0), axis=0, keepdims=True)
         xs[strided(i), :] = (
             gg[pl.ds(i * blocks, blocks), :] + joined(rest[i], w_back[i])[:blocks]
         )
@@ -386,6 +416,10 @@
     finish_stream(2, grad_gated * conv(1), gkvs, 1)
     give(gkvs, gkvb, 1)
 
+    for i in range(OWN):
+        pair = dot(xr[strided(i), :].astype(BF16), gs[strided(i), :].astype(BF16), 0, 0)
+        turned = pltpu.roll(pair, 1, 1, stride=1, stride_axis=0)
+        cd[pl.ds(i, 1), :] = jnp.sum(jnp.where(lane2 <= row2, turned, 0.0), axis=0, keepdims=True)
     corr = cd[...][:, None, :] * near
     by_res = jnp.sum(corr + t0 * state, axis=2, keepdims=True)
     by_rate = jnp.sum(corr * time + t1 * state + t0 * d_state, axis=2, keepdims=True)
@@ -396,7 +430,7 @@
         jnp.where(lane3 == 16 + mode3, by_res, jnp.where(lane3 == 32 + mode3, by_log, 0.0)), axis=1
     )
     for j, total in enumerate(sums):
-        tiny = jnp.where(lane == j, total, tiny)
+        tiny = jnp.where(lane == j, jnp.sum(total, axis=1, keepdims=True), tiny)
     smalls[...] = jnp.where(lane[:8] < BLK // 2, tiny[:8], pltpu.roll(tiny[8:], BLK // 2, 1))
 
     @pl.loop(1, POS)
@@ -406,7 +440,7 @@
 
     smallb[p] = smalls[...]
 
-    for copy in first + weights + [share, across] + hops + shared:
+    for copy in first + weights + [share] + across + hops + shared:
         copy.wait_send()
     for sem, (ref, out) in enumerate(((gqb, gq_out), (gkvb, gkv_out), (smallb, small_out))):
         remote(ref.at[rest_slots], ref.at[rest_slots], os.at[sem], orr.at[sem], pos=sibling).wait()
@@ -435,8 +469,8 @@
             pltpu.VMEM((chans, ROW * cols), BF16),
             pltpu.VMEM((YH, 16, half), BF16),
             pltpu.VMEM((CHAN, YH, 16, half), BF16),
-            pltpu.VMEM((GROUPS, POS, OWN, BLK), BF16),
-            pltpu.VMEM((GROUPS, POS, OWN, BLK), BF16),
+            pltpu.VMEM((POS, GROUPS, OWN, BLK), BF16),
+            pltpu.VMEM((POS, GROUPS, OWN, BLK), BF16),
             pltpu.VMEM((GROUPS * BLK, GROUPS * BLK), BF16),
         ]
         + [pltpu.VMEM((rows, BLK), F32)] * 5
@@ -449,23 +483,32 @@
             dma, dma,
             dma((YH - 1,)), dma((YH - 1,)),
             dma((7,)), dma((7,)),
-            dma, dma,
-            dma((CHAN,)), dma((CHAN,)),
-            dma((GROUPS,)), dma((GROUPS,)),
+            dma((YH,)), dma((YH,)),
+            dma((CHAN * YH,)), dma((CHAN * YH,)),
+            dma((len(PARTS),)), dma((len(PARTS),)),
             dma((3,)), dma((3,)),
         ],
         compiler_params=pltpu.CompilerParams(
-            collective_id=0, has_side_effects=True, vmem_limit_bytes=48 * 1024 * 1024
+            collective_id=0, has_side_effects=True, vmem_limit_bytes=VMEM
         ),
         name="mixer",
     )(q, k, v, short_weights, residues, log_decay, w, g)
 
 
-def finish_kernel(gq, gkv, small, q, k, v, short, res, dec):
+def finish_kernel(gq_in, gkv_in, small_in, q, k, v, short, res, dec, gq, gkv, small, local):
     chans = POS * OWN
+    loads = [
+        pltpu.make_async_copy(src, dst, local.at[i])
+        for i, (src, dst) in enumerate([(gq_in, gq), (gkv_in, gkv), (small_in, small)])
+    ]
+    for copy in loads:
+        copy.start()
+    loads[0].wait()
     q[...] = gq[...].astype(F32).reshape(chans, BLK).T.astype(BF16)
+    loads[1].wait()
     for s, ref in enumerate((k, v)):
         ref[...] = gkv[:, s].astype(F32).reshape(chans, BLK).T.astype(BF16)
+    loads[2].wait()
     packed = small[...]
     both = jnp.concatenate([packed, pltpu.roll(packed, BLK // 2, 2)], axis=1)
     turned = both.reshape(chans, BLK).T
@@ -482,9 +525,11 @@
     return pl.pallas_call(
         finish_kernel,
         out_shape=(stream, stream, stream, jax.ShapeDtypeStruct((3, TAPS, chans), F32), mode, mode),
-        in_specs=[full()] * 3,
+        in_specs=[full(pl.ANY)] * 3,
         out_specs=(full(),) * 6,
-        compiler_params=pltpu.CompilerParams(vmem_limit_bytes=48 * 1024 * 1024),
+        scratch_shapes=[pltpu.VMEM(a.shape, a.dtype) for a in (gq, gkv, small)]
+        + [pltpu.SemaphoreType.DMA((3,))],
+        compiler_params=pltpu.CompilerParams(vmem_limit_bytes=VMEM),
         name="finish",
     )(gq, gkv, small)
 

time: 85.1 us -> 77.3 us (0.908)
  local copies, waits for them, and re-layouts: 6.81 us -> 0 us
    unnamed x16 -> x0, local copies, waits for them, and re-layouts: 6.81 us -> none
    pallas_call x1, Pallas kernels: 76.3 us -> 74.5 us  [mixer(): pl.pallas_call(mixer_kernel, out_shape=tuple((jax.ShapeDtypeStruct(*o) fo...]
    pallas_call x1, Pallas kernels: 0.92 us -> 2.01 us  [finish(): pl.pallas_call(finish_kernel, out_shape=(stream, stream, stream, jax.Shap...]
where the time goes in v3:
time: 77.3 us; the launch traced here: 77.2 us
  Pallas kernels  76.5 us (99%)
    pallas_call x1, Pallas kernels, mixer(): pl.pallas_call(mixer_kernel, out_shape=tuple((jax.ShapeDtypeStruct(*o) fo...  74.5 us
    pallas_call x1, Pallas kernels, finish(): pl.pallas_call(finish_kernel, out_shape=(stream, stream, stream, jax.Shap...  2.01 us

profile of v3, /device:TPU:1, one launch (start us, length us, event | category | flops | bytes accessed | tf_op | source)
XLA Modules:
  0.0 77.2 jit_solution(1849904872788312560)
XLA Ops:
  0.6 74.5 %mixer.1 = (bf16[32,16,128]{2,1,0:T(8,128)(2,1)}, bf16[32,2,16,128]{3,2,1,0:T(8,128)(2,1)}, f32[32,8,128]{2,1,0:T(8,128)}) custom-call(bf16[128,512]{1,0:T(8,128)(2,1)} %q.1, bf16[128,512]{1,0:T(8,128)(2,1)} %k.1, bf16[128,512]{1,0:T(8,128)(2,1)} %v.1, f32[3,3,512]{2,1,0:T(4,128)} %sw.1, f32[16,512]{1,0:T(8,128)} %bitcast.4, f32[16,512]{1,0:T(8,128)} %bitcast.5, ...), custom_call_target="tpu_custom_call" | custom-call | tf_op jit(solution)/shard_map/mixer/pallas_call | solution.py:456
  75.2 2.0 %finish.1 = (bf16[128,512]{1,0:T(8,128)(2,1)}, bf16[128,512]{1,0:T(8,128)(2,1)}, bf16[128,512]{1,0:T(8,128)(2,1)}, f32[3,3,512]{2,1,0:T(4,128)}, f32[16,512]{1,0:T(8,128)}, /*index=5*/f32[16,512]{1,0:T(8,128)}) custom-call(bf16[32,16,128]{2,1,0:T(8,128)(2,1)} %get-tuple-element.15.gq_in, bf16[32,2,16,128]{3,2,1,0:T(8,128)(2,1)} %get-tuple-element.16.gkv_in, ...), custom_call_target="tpu_custom_call" | custom-call | tf_op jit(solution)/shard_map/finish/pallas_call | solution.py:525

commit v4 on v3

--- a/solution.py
+++ b/solution.py
@@ -262,7 +262,6 @@
 
     arrive(0, 1)
     arrive(1, 1)
-    remote(slab.at[rest_slots], inb.at[rest_slots], qs, qr, pos=sibling).wait()
     blocks = POS
     rows = blocks * OWN
     shape = (blocks, OWN, BLK)
@@ -282,6 +281,7 @@
         return pl.ds(i, blocks, stride=OWN)
 
     def gate():
+        remote(slab.at[rest_slots], inb.at[rest_slots], qs, qr, pos=sibling).wait()
         xs[...] = (conv(1) * conv(2)).astype(BF16).astype(F32).reshape(rows, BLK)
 
     def within(low, high):
@@ -343,12 +343,18 @@
         product(0)
 
     half_own = OWN // 2
+    arrive(0, 2)
     for i in (1, 3, 2):
         share_weights(i)
-    arrive(0, 2, gate, within(0, 5), within(5, 11), within(11, OWN))
-    arrive(1, 2, weights_in, lambda: product(1), lambda: give_part(0), edges)
-    arrive(0, 3, between(0, half_own), between(half_own, OWN), order)
-    arrive(1, 3, lambda: product(2), lambda: give_part(1))
+    arrive(1, 2, weights_in, lambda: product(1), lambda: give_part(0))
+    arrive(0, 3, order)
+    arrive(1, 3)
+    product(2)
+    give_part(1)
+    gate()
+    within(0, OWN)()
+    edges()
+    between(0, OWN)()
     for r in range(YH):
         for sel, way, hop in ORDER[-2:]:
             ring(way, sel, hop, r).wait_recv()
@@ -382,13 +388,14 @@
         for j in range(TAPS):
             sums.append(jnp.sum(grad * later(values, j), axis=0))
 
-    def give(mine_ref, all_ref, sem):
+    def give(mine_ref, all_ref, sem, *index):
         @pl.loop(1, POS)
         def _(i):
             to = (p + i) % POS
-            remote(mine_ref.at[to], all_ref.at[p], os.at[sem], orr.at[sem], pos=to).start()
-
-        all_ref[p] = mine_ref[p]
+            remote(mine_ref.at[(to, *index)], all_ref.at[(p, *index)], os.at[sem], orr.at[sem],
+                   pos=to).start()
+
+        all_ref[(p, *index)] = mine_ref[(p, *index)]
 
     finish_stream(0, mix * xs[...].reshape(shape), gqs, None)
     give(gqs, gqb, 0)
@@ -413,8 +420,8 @@
         )
     grad_gated = xs[...].reshape(shape)
     finish_stream(1, grad_gated * conv(2), gkvs, 0)
+    give(gkvs, gkvb, 1, 0)
     finish_stream(2, grad_gated * conv(1), gkvs, 1)
-    give(gkvs, gkvb, 1)
 
     for i in range(OWN):
         pair = dot(xr[strided(i), :].astype(BF16), gs[strided(i), :].astype(BF16), 0, 0)
@@ -433,18 +440,29 @@
         tiny = jnp.where(lane == j, jnp.sum(total, axis=1, keepdims=True), tiny)
     smalls[...] = jnp.where(lane[:8] < BLK // 2, tiny[:8], pltpu.roll(tiny[8:], BLK // 2, 1))
 
-    @pl.loop(1, POS)
+    for i in range(1, YH):
+        to = ((h + i) % YH) * ROW + mine
+        remote(smalls, smallb.at[mine, h], os.at[3], orr.at[3], pos=to).start()
+    smallb[mine, h] = smalls[...]
+    give(gkvs, gkvb, 2, 1)
+    three = smallb.at[0, pl.ds(0, YH - 1)]
+    remote(three, three, os.at[3], orr.at[3], pos=sibling).wait()
+
+    @pl.loop(1, ROW)
     def _(i):
-        to = (p + i) % POS
-        remote(smalls, smallb.at[p], os.at[2], orr.at[2], pos=to).start()
-
-    smallb[p] = smalls[...]
+        to = h * ROW + (mine + i) % ROW
+        remote(smallb.at[mine], smallb.at[mine], os.at[4], orr.at[4], pos=to).start()
 
     for copy in first + weights + [share] + across + hops + shared:
         copy.wait_send()
-    for sem, (ref, out) in enumerate(((gqb, gq_out), (gkvb, gkv_out), (smallb, small_out))):
-        remote(ref.at[rest_slots], ref.at[rest_slots], os.at[sem], orr.at[sem], pos=sibling).wait()
-        out[...] = ref[...]
+    gkv_rest = [gkvb.at[rest_slots, i] for i in (0, 1)]
+    for sem, ref in enumerate((gqb.at[rest_slots], *gkv_rest)):
+        remote(ref, ref, os.at[sem], orr.at[sem], pos=sibling).wait()
+    gq_out[...] = gqb[...]
+    gkv_out[...] = gkvb[...]
+    seven = smallb.at[pl.ds(0, ROW - 1)]
+    remote(seven, seven, os.at[4], orr.at[4], pos=sibling).wait()
+    small_out[...] = smallb[...]
 
 
 def mixer(q, k, v, short_weights, residues, log_decay, w, g):
@@ -452,7 +470,7 @@
     dma = pltpu.SemaphoreType.DMA
     half = g.shape[1] // YH // 2
     rows = POS * OWN
-    outs = [((POS, OWN, BLK), BF16), ((POS, 2, OWN, BLK), BF16), ((POS, 8, BLK), F32)]
+    outs = [((POS, OWN, BLK), BF16), ((POS, 2, OWN, BLK), BF16), ((ROW, YH, 8, BLK), F32)]
     return pl.pallas_call(
         mixer_kernel,
         out_shape=tuple(jax.ShapeDtypeStruct(*o) for o in outs),
@@ -486,7 +504,7 @@
             dma((YH,)), dma((YH,)),
             dma((CHAN * YH,)), dma((CHAN * YH,)),
             dma((len(PARTS),)), dma((len(PARTS),)),
-            dma((3,)), dma((3,)),
+            dma((5,)), dma((5,)),
         ],
         compiler_params=pltpu.CompilerParams(
             collective_id=0, has_side_effects=True, vmem_limit_bytes=VMEM
@@ -510,8 +528,8 @@
         ref[...] = gkv[:, s].astype(F32).reshape(chans, BLK).T.astype(BF16)
     loads[2].wait()
     packed = small[...]
-    both = jnp.concatenate([packed, pltpu.roll(packed, BLK // 2, 2)], axis=1)
-    turned = both.reshape(chans, BLK).T
+    both = jnp.concatenate([packed, pltpu.roll(packed, BLK // 2, 3)], axis=2)
+    turned = jnp.concatenate([both[:, i] for i in range(YH)], axis=0).reshape(chans, BLK).T
     res[...] = turned[16:32]
     dec[...] = turned[32:48]
     for s in range(3):

time: 77.3 us -> 73.8 us (0.955)
  Pallas kernels: 76.5 us -> 73 us
    pallas_call x1, Pallas kernels: 74.5 us -> 71 us  [mixer(): pl.pallas_call(mixer_kernel, out_shape=tuple((jax.ShapeDtypeStruct(*o) fo...]
where the time goes in v4:
time: 73.8 us; the launch traced here: 73.6 us
  Pallas kernels  73 us (99%)
    pallas_call x1, Pallas kernels, mixer(): pl.pallas_call(mixer_kernel, out_shape=tuple((jax.ShapeDtypeStruct(*o) fo...  71 us
    pallas_call x1, Pallas kernels, finish(): pl.pallas_call(finish_kernel, out_shape=(stream, stream, stream, jax.Shap...  2 us

profile of v4, /device:TPU:1, one launch (start us, length us, event | category | flops | bytes accessed | tf_op | source)
XLA Modules:
  0.0 73.6 jit_solution(13005304072527380064)
XLA Ops:
  0.6 71.0 %mixer.1 = (bf16[32,16,128]{2,1,0:T(8,128)(2,1)}, bf16[32,2,16,128]{3,2,1,0:T(8,128)(2,1)}, f32[8,4,8,128]{3,2,1,0:T(8,128)}) custom-call(bf16[128,512]{1,0:T(8,128)(2,1)} %q.1, bf16[128,512]{1,0:T(8,128)(2,1)} %k.1, bf16[128,512]{1,0:T(8,128)(2,1)} %v.1, f32[3,3,512]{2,1,0:T(4,128)} %sw.1, f32[16,512]{1,0:T(8,128)} %bitcast.4, f32[16,512]{1,0:T(8,128)} %bitcast.5, ...), custom_call_target="tpu_custom_call" | custom-call | tf_op jit(solution)/shard_map/mixer/pallas_call | solution.py:474
  71.6 2.0 %finish.1 = (bf16[128,512]{1,0:T(8,128)(2,1)}, bf16[128,512]{1,0:T(8,128)(2,1)}, bf16[128,512]{1,0:T(8,128)(2,1)}, f32[3,3,512]{2,1,0:T(4,128)}, f32[16,512]{1,0:T(8,128)}, /*index=5*/f32[16,512]{1,0:T(8,128)}) custom-call(bf16[32,16,128]{2,1,0:T(8,128)(2,1)} %get-tuple-element.15.gq_in, bf16[32,2,16,128]{3,2,1,0:T(8,128)(2,1)} %get-tuple-element.16.gkv_in, ...), custom_call_target="tpu_custom_call" | custom-call | tf_op jit(solution)/shard_map/finish/pallas_call | solution.py:543

commit v5 on v4

--- a/solution.py
+++ b/solution.py
@@ -174,13 +174,6 @@
         first[s].wait_recv()
         pass_own(s + 1)
 
-    @pl.loop(1, POS)
-    def _(i):
-        to = (p + i) % POS
-        remote(slab.at[to], inb.at[p], qs, qr, pos=to).start()
-
-    inb[p] = slab[p]
-
     shared = []
 
     def share_weights(i):
@@ -214,7 +207,7 @@
 
         @pl.loop(1, POS)
         def _(i):
-            to = (p + i) % POS
+            to = (p + (i + 7) % (POS - 1) + 1) % POS
             remote(pout.at[to, tiles], pin.at[p, tiles], ps.at[part], pr.at[part], pos=to).start()
 
         pin[p, tiles] = pout[p, tiles]
@@ -224,41 +217,12 @@
         send(0, 1, 1, r)
         send(1, 1, 1, r)
 
-    for copy in loads[5:]:
-        copy.wait()
-    chans = swv.shape[2]
-    pick = lax.broadcasted_iota(jnp.int32, (OWN, chans), 1) == (
-        first_chan + lax.broadcasted_iota(jnp.int32, (OWN, chans), 0)
-    )
-    taps_of = [
-        [
-            jnp.sum(jnp.where(pick, swv[s, pl.ds(j, 1), :], 0.0), axis=1, keepdims=True)[None]
-            for j in range(TAPS)
-        ]
-        for s in range(3)
-    ]
-    eye = (
-        lax.broadcasted_iota(jnp.int32, (OWN, MODES, MODES), 1)
-        == lax.broadcasted_iota(jnp.int32, (OWN, MODES, MODES), 2)
-    )
-
-    def columns(ref):
-        own = pltpu.roll(ref[...], chans - first_chan, 1)[:, :BLK].T[:OWN]
-        spread = jnp.where(eye, jnp.broadcast_to(own[:, None, :], eye.shape), 0.0)
-        return jnp.sum(spread, axis=2, keepdims=True)
-
-    shape3 = (OWN, MODES, BLK)
-    time = lax.broadcasted_iota(jnp.int32, shape3, 2).astype(F32)
-    weight = jnp.broadcast_to(columns(resv), shape3)
-    rate = jnp.exp(jnp.broadcast_to(columns(ldv), shape3))
-    near = jnp.exp(-rate * time)
-    ahead = jnp.exp(-rate * (time + 1.0))
-    back = jnp.exp(-rate * (BLK - 1.0 - time))
-    taps = jnp.sum(weight * near, axis=1)
-    t_ahead = (time + 1.0) * ahead
-    t_back = (BLK - 1.0 - time) * back
-    w_ahead = weight * ahead
-    w_back = weight * back
+    @pl.loop(1, POS)
+    def _(i):
+        to = (p + i) % POS
+        remote(slab.at[to], inb.at[p], qs, qr, pos=to).start()
+
+    inb[p] = slab[p]
 
     arrive(0, 1)
     arrive(1, 1)
@@ -346,11 +310,48 @@
     arrive(0, 2)
     for i in (1, 3, 2):
         share_weights(i)
-    arrive(1, 2, weights_in, lambda: product(1), lambda: give_part(0))
-    arrive(0, 3, order)
+    arrive(1, 2)
+    arrive(0, 3, weights_in, lambda: product(1), lambda: give_part(0), order)
     arrive(1, 3)
     product(2)
     give_part(1)
+
+    for copy in loads[5:]:
+        copy.wait()
+    chans = swv.shape[2]
+    pick = lax.broadcasted_iota(jnp.int32, (OWN, chans), 1) == (
+        first_chan + lax.broadcasted_iota(jnp.int32, (OWN, chans), 0)
+    )
+    taps_of = [
+        [
+            jnp.sum(jnp.where(pick, swv[s, pl.ds(j, 1), :], 0.0), axis=1, keepdims=True)[None]
+            for j in range(TAPS)
+        ]
+        for s in range(3)
+    ]
+    eye = (
+        lax.broadcasted_iota(jnp.int32, (OWN, MODES, MODES), 1)
+        == lax.broadcasted_iota(jnp.int32, (OWN, MODES, MODES), 2)
+    )
+
+    def columns(ref):
+        own = pltpu.roll(ref[...], chans - first_chan, 1)[:, :BLK].T[:OWN]
+        spread = jnp.where(eye, jnp.broadcast_to(own[:, None, :], eye.shape), 0.0)
+        return jnp.sum(spread, axis=2, keepdims=True)
+
+    shape3 = (OWN, MODES, BLK)
+    time = lax.broadcasted_iota(jnp.int32, shape3, 2).astype(F32)
+    weight = jnp.broadcast_to(columns(resv), shape3)
+    rate = jnp.exp(jnp.broadcast_to(columns(ldv), shape3))
+    near = jnp.exp(-rate * time)
+    ahead = jnp.exp(-rate * (time + 1.0))
+    back = jnp.exp(-rate * (BLK - 1.0 - time))
+    taps = jnp.sum(weight * near, axis=1)
+    t_ahead = (time + 1.0) * ahead
+    t_back = (BLK - 1.0 - time) * back
+    w_ahead = weight * ahead
+    w_back = weight * back
+
     gate()
     within(0, OWN)()
     edges()
@@ -391,7 +392,7 @@
     def give(mine_ref, all_ref, sem, *index):
         @pl.loop(1, POS)
         def _(i):
-            to = (p + i) % POS
+            to = (p + (i + 7) % (POS - 1) + 1) % POS
             remote(mine_ref.at[(to, *index)], all_ref.at[(p, *index)], os.at[sem], orr.at[sem],
                    pos=to).start()
 

time: 73.8 us -> 73.1 us (level)
  no operation moved by 1% of the time
where the time goes in v5:
time: 73.1 us; the launch traced here: 73 us
  Pallas kernels  72.3 us (99%)
    pallas_call x1, Pallas kernels, mixer(): pl.pallas_call(mixer_kernel, out_shape=tuple((jax.ShapeDtypeStruct(*o) fo...  70.3 us
    pallas_call x1, Pallas kernels, finish(): pl.pallas_call(finish_kernel, out_shape=(stream, stream, stream, jax.Shap...  2 us

profile of v5, /device:TPU:1, one launch (start us, length us, event | category | flops | bytes accessed | tf_op | source)
XLA Modules:
  0.0 73.0 jit_solution(11495109596330379187)
XLA Ops:
  0.6 70.3 %mixer.1 = (bf16[32,16,128]{2,1,0:T(8,128)(2,1)}, bf16[32,2,16,128]{3,2,1,0:T(8,128)(2,1)}, f32[8,4,8,128]{3,2,1,0:T(8,128)}) custom-call(bf16[128,512]{1,0:T(8,128)(2,1)} %q.1, bf16[128,512]{1,0:T(8,128)(2,1)} %k.1, bf16[128,512]{1,0:T(8,128)(2,1)} %v.1, f32[3,3,512]{2,1,0:T(4,128)} %sw.1, f32[16,512]{1,0:T(8,128)} %bitcast.4, f32[16,512]{1,0:T(8,128)} %bitcast.5, ...), custom_call_target="tpu_custom_call" | custom-call | tf_op jit(solution)/shard_map/mixer/pallas_call | solution.py:475
  71.0 2.0 %finish.1 = (bf16[128,512]{1,0:T(8,128)(2,1)}, bf16[128,512]{1,0:T(8,128)(2,1)}, bf16[128,512]{1,0:T(8,128)(2,1)}, f32[3,3,512]{2,1,0:T(4,128)}, f32[16,512]{1,0:T(8,128)}, /*index=5*/f32[16,512]{1,0:T(8,128)}) custom-call(bf16[32,16,128]{2,1,0:T(8,128)(2,1)} %get-tuple-element.15.gq_in, bf16[32,2,16,128]{3,2,1,0:T(8,128)(2,1)} %get-tuple-element.16.gkv_in, ...), custom_call_target="tpu_custom_call" | custom-call | tf_op jit(solution)/shard_map/finish/pallas_call | solution.py:544
